TPU v7x, 128 devices: a whole 4x4x4 slice. The times are simulated.
128 devices in a mesh: node: 8 (over x, core), rail: 16 (over z, y).
Axes of the slice: x: 4, y: 4, z: 4, core: 2. Of those that a mesh axis runs over, the one named last changes fastest.
Arguments:
- tokens: bfloat16 [8192, 2048], P(('node', 'rail')), may hold values from -6 to 6
- routes: int32 [8192, 8], P(('node', 'rail')), may hold values from 0 to 127, all different within a row; in each aligned block of 64 rows (0 to 63, 64 to 127, ...) at most 8 rows name the same one
- route_weights: float32 [8192, 8], P(('node', 'rail')), may hold values from 0.03 to 0.4
- cotangent: bfloat16 [8192, 2048], P(('node', 'rail')), may hold values from -6 to 6
- gate_weight: bfloat16 [128, 2048, 768], P(('node', 'rail')), may hold values from -0.125 to 0.125
- up_weight: bfloat16 [128, 2048, 768], P(('node', 'rail')), may hold values from -0.125 to 0.125
- down_weight: bfloat16 [128, 768, 2048], P(('node', 'rail')), may hold values from -0.21875 to 0.21875
Outputs:
- mixed: bfloat16 [8192, 2048], P(('node', 'rail'))
- token_grad: bfloat16 [8192, 2048], P(('node', 'rail'))
- weight_grad: float32 [8192, 8], P(('node', 'rail'))
- gate_grad: bfloat16 [128, 2048, 768], P(('node', 'rail'))
- up_grad: bfloat16 [128, 2048, 768], P(('node', 'rail'))
- down_grad: bfloat16 [128, 768, 2048], P(('node', 'rail'))
Inputs may be any that keep to these rules, and one draw needn't show every extreme that they name: `routes`: each token names 8 different experts. Among the tokens of one block of 64 consecutive tokens no expert is named more than 8 times, and in every draw some expert is named exactly 8 times by one block.
All inputs are finite; a program needn't handle non-finite values.
Results may differ from a plain program's by a relative error of at most 0.0064.
Values may be sent and summed in bfloat16 or wider, within the bound.
A program may use at most 128 MiB of HBM per device.

v0:
```python
import jax
import jax.numpy as jnp
from jax import lax
from jax.sharding import PartitionSpec as P


def expert_forward(slot_rows, w_gate, w_up, w_down):
    gate_pre = jnp.dot(slot_rows, w_gate, preferred_element_type=jnp.float32)
    up_pre = jnp.dot(slot_rows, w_up, preferred_element_type=jnp.float32)
    hidden = (jax.nn.silu(gate_pre) * up_pre).astype(jnp.bfloat16)
    output = jnp.dot(hidden, w_down, preferred_element_type=jnp.float32).astype(jnp.bfloat16)
    return (gate_pre, up_pre, hidden, output)


def expert_backward(slot_rows, slot_grads, gate_pre, up_pre, hidden, w_gate, w_up, w_down):
    contract_last = (((1,), (1,)), ((), ()))
    contract_first = (((0,), (0,)), ((), ()))
    hidden_back = lax.dot_general(
        slot_grads, w_down, contract_last, preferred_element_type=jnp.float32
    )
    sigmoid_gate = jax.nn.sigmoid(gate_pre)
    gate_back = (
        hidden_back * up_pre * sigmoid_gate * (1.0 + gate_pre * (1.0 - sigmoid_gate))
    ).astype(jnp.bfloat16)
    up_back = (hidden_back * gate_pre * sigmoid_gate).astype(jnp.bfloat16)
    down_grad = lax.dot_general(
        hidden, slot_grads, contract_first, preferred_element_type=jnp.float32
    ).astype(jnp.bfloat16)
    gate_grad = lax.dot_general(
        slot_rows, gate_back, contract_first, preferred_element_type=jnp.float32
    ).astype(jnp.bfloat16)
    up_grad = lax.dot_general(
        slot_rows, up_back, contract_first, preferred_element_type=jnp.float32
    ).astype(jnp.bfloat16)
    input_back = lax.dot_general(
        gate_back, w_gate, contract_last, preferred_element_type=jnp.float32
    )
    input_back = input_back + lax.dot_general(
        up_back, w_up, contract_last, preferred_element_type=jnp.float32
    )
    return (input_back.astype(jnp.bfloat16), gate_grad, up_grad, down_grad)


def combine_slots(out_slot, back_slot, route_weights, cotangent):
    out_float = out_slot.astype(jnp.float32)
    mixed = jnp.einsum(
        "tk,tkd->td", route_weights, out_float, precision=lax.Precision.HIGHEST
    ).astype(jnp.bfloat16)
    weight_grad = jnp.einsum(
        "tkd,td->tk", out_float, cotangent.astype(jnp.float32), precision=lax.Precision.HIGHEST
    )
    token_grad = jnp.sum(back_slot.astype(jnp.float32), axis=1).astype(jnp.bfloat16)
    return (mixed, token_grad, weight_grad)


def per_device(tokens, routes, route_weights, cotangent, gate_weight, up_weight, down_weight):
    token_count, model_width = tokens.shape
    top_count = routes.shape[1]
    experts = lax.axis_size(("node", "rail"))
    capacity = 2 * token_count * top_count // experts
    flat_routes = routes.reshape(-1)
    onehot = (flat_routes[:, None] == jnp.arange(experts, dtype=jnp.int32)[None, :]).astype(
        jnp.int32
    )
    position = jnp.sum((jnp.cumsum(onehot, axis=0) - onehot) * onehot, axis=1)
    slot_index = flat_routes * capacity + position
    total_slots = experts * capacity
    owner_row = (
        jnp.zeros((total_slots,), jnp.int32)
        .at[slot_index]
        .set(jnp.arange(token_count * top_count, dtype=jnp.int32))
    )
    filled = (
        jnp.zeros((total_slots,), jnp.int32)
        .at[slot_index]
        .set(jnp.ones((token_count * top_count,), jnp.int32))
    )
    token_of = owner_row // top_count
    weight_of = route_weights.reshape(-1)[owner_row]
    keep_mask = (filled > 0)[:, None]
    send_rows = jnp.where(keep_mask, tokens[token_of], jnp.zeros((), jnp.bfloat16)).reshape(
        experts, capacity, model_width
    )
    send_grads = (
        jnp.where(
            keep_mask,
            weight_of[:, None] * cotangent[token_of].astype(jnp.float32),
            jnp.float32(0.0),
        )
        .astype(jnp.bfloat16)
        .reshape(experts, capacity, model_width)
    )
    w_gate = gate_weight[0]
    w_up = up_weight[0]
    w_down = down_weight[0]
    recv_rows = lax.all_to_all(send_rows, ("node", "rail"), split_axis=0, concat_axis=0, tiled=True)
    slot_rows = recv_rows.reshape(-1, model_width)
    gate_pre, up_pre, hidden, output = expert_forward(slot_rows, w_gate, w_up, w_down)
    out_home = lax.all_to_all(
        output.reshape(experts, capacity, model_width),
        ("node", "rail"),
        split_axis=0,
        concat_axis=0,
        tiled=True,
    )
    recv_grads = lax.all_to_all(
        send_grads, ("node", "rail"), split_axis=0, concat_axis=0, tiled=True
    )
    slot_grads = recv_grads.reshape(-1, model_width)
    input_back, gate_grad, up_grad, down_grad = expert_backward(
        slot_rows, slot_grads, gate_pre, up_pre, hidden, w_gate, w_up, w_down
    )
    back_home = lax.all_to_all(
        input_back.reshape(experts, capacity, model_width),
        ("node", "rail"),
        split_axis=0,
        concat_axis=0,
        tiled=True,
    )
    out_slot = out_home.reshape(-1, model_width)[slot_index].reshape(
        token_count, top_count, model_width
    )
    back_slot = back_home.reshape(-1, model_width)[slot_index].reshape(
        token_count, top_count, model_width
    )
    mixed, token_grad, weight_grad = combine_slots(out_slot, back_slot, route_weights, cotangent)
    return (mixed, token_grad, weight_grad, gate_grad[None], up_grad[None], down_grad[None])


def solution(mesh):
    placed = (
        P(("node", "rail"), None),
        P(("node", "rail"), None),
        P(("node", "rail"), None),
        P(("node", "rail"), None),
        P(("node", "rail"), None, None),
        P(("node", "rail"), None, None),
        P(("node", "rail"), None, None),
    )
    return jax.shard_map(
        per_device,
        mesh=mesh,
        in_specs=placed,
        out_specs=(
            P(("node", "rail"), None),
            P(("node", "rail"), None),
            P(("node", "rail"), None),
            P(("node", "rail"), None, None),
            P(("node", "rail"), None, None),
            P(("node", "rail"), None, None),
        ),
        check_vma=False,
    )
```

profile of v0, /device:TPU:7, one launch (start us, length us, event | category | flops | bytes accessed | tf_op | source)
XLA Modules:
  0.0 284.7 jit_solution(9509259095651761206)
XLA Ops:
  1.5 0.9 copy.14
  3.9 1.0 broadcast_add_fusion
  5.1 2.4 scatter_custom_fusion.1
  7.6 2.4 scatter_custom_fusion
  10.2 6.0 %gather_fusion = bf16[1024,2048]{1,0:T(8,128)(2,1)} fusion(bf16[64,2048]{1,0:T(8,128)(2,1)S(1)} %copy-done.2, s32[1024]{0:T(1024)S(1)} %get-tuple-element.10), kind=kCustom, calls=%fused_computation | custom fusion | bytes 8392704 | tf_op jit(solution)/shard_map/gather | solution.py:81
  16.2 4.5 %bitcast_select_fusion = bf16[128,8,2048]{2,1,0:T(8,128)(2,1)} fusion(bf16[1024,2048]{1,0:T(8,128)(2,1)} %gather_fusion, pred[128,8]{1,0:T(8,128)(4,1)S(1)} %broadcast_in_dim.51), kind=kLoop, calls=%fused_computation.24 | loop fusion | flops 2097152 | bytes 8389632 | tf_op jit(solution)/shard_map/jit(_where)/select_n | solution.py:81
  20.7 11.2 %all-to-all-start = ((bf16[128,8,2048]{2,1,0:T(8,128)(2,1)}), bf16[128,8,2048]{2,1,0:T(8,128)(2,1)}, u32[]{:S(2)}, u32[]{:S(2)}) async-start(bf16[128,8,2048]{2,1,0:T(8,128)(2,1)} %bitcast_select_fusion), calls=%async_computation | async-start | bytes 8388608 | tf_op jit(solution)/shard_map/all_to_all | solution.py:96
  32.2 6.9 %gather_fusion.2 = f32[1024]{0:T(1024)S(1)} fusion(f32[512]{0:T(512)S(1)} %reshape.112, s32[1024]{0:T(1024)S(1)} %get-tuple-element.9), kind=kCustom, calls=%fused_computation.2 | custom fusion | bytes 12288 | tf_op jit(solution)/shard_map/gather | solution.py:79
  39.1 6.0 %gather_fusion.3 = bf16[1024,2048]{1,0:T(8,128)(2,1)} fusion(bf16[64,2048]{1,0:T(8,128)(2,1)S(1)} %copy-done.3, s32[1024]{0:T(1024)S(1)} %get-tuple-element.10), kind=kCustom, calls=%fused_computation.3 | custom fusion | bytes 8392704 | tf_op jit(solution)/shard_map/gather | solution.py:87
  45.2 4.1 %fusion.1 = bf16[128,8,2048]{2,1,0:T(8,128)(2,1)} fusion(bf16[1024,2048]{1,0:T(8,128)(2,1)} %gather_fusion.3, f32[128,8]{1,0:T(8,128)S(1)} %mul.61, pred[128,8]{1,0:T(8,128)(4,1)S(1)} %broadcast_in_dim.51), kind=kLoop, calls=%fused_computation.9 | loop fusion | flops 8388608 | bytes 8393728 | tf_op jit(solution)/shard_map/convert_element_type | solution.py:90
  49.3 34.6 %all-to-all-done = bf16[128,8,2048]{2,1,0:T(8,128)(2,1)} async-done(((bf16[128,8,2048]{2,1,0:T(8,128)(2,1)}), bf16[128,8,2048]{2,1,0:T(8,128)(2,1)}, u32[]{:S(2)}, u32[]{:S(2)}) %all-to-all-start) | async-done | bytes 4194336 | tf_op jit(solution)/shard_map/all_to_all | solution.py:96
  83.9 5.8 %all-to-all-start.2 = ((bf16[128,8,2048]{2,1,0:T(8,128)(2,1)}), bf16[128,8,2048]{2,1,0:T(8,128)(2,1)}, u32[]{:S(2)}, u32[]{:S(2)}) async-start(bf16[128,8,2048]{2,1,0:T(8,128)(2,1)} %fusion.1), calls=%async_computation.2 | async-start | bytes 8388608 | tf_op jit(solution)/shard_map/all_to_all | solution.py:106
  89.8 8.4 %fusion.11 = f32[1024,768]{1,0:T(8,128)} fusion(bf16[128,8,2048]{2,1,0:T(8,128)(2,1)} %all-to-all-done, bf16[1,2048,768]{2,1,0:T(8,128)(2,1)} %param.12), kind=kOutput, calls=%fused_computation.20 | convolution fusion | flops 3221225472 | bytes 10485760 | tf_op jit(solution)/shard_map/dot_general | solution.py:9
  98.1 7.3 %fusion.13 = f32[1024,768]{1,0:T(8,128)} fusion(bf16[128,8,2048]{2,1,0:T(8,128)(2,1)} %all-to-all-done, bf16[1,2048,768]{2,1,0:T(8,128)(2,1)S(1)} %copy-done.6), kind=kOutput, calls=%fused_computation.22 | convolution fusion | flops 3221225472 | bytes 10485760 | tf_op jit(solution)/shard_map/dot_general | solution.py:8
  105.4 36.1 %all-to-all-done.2 = bf16[128,8,2048]{2,1,0:T(8,128)(2,1)} async-done(((bf16[128,8,2048]{2,1,0:T(8,128)(2,1)}), bf16[128,8,2048]{2,1,0:T(8,128)(2,1)}, u32[]{:S(2)}, u32[]{:S(2)}) %all-to-all-start.2) | async-done | bytes 4194336 | tf_op jit(solution)/shard_map/all_to_all | solution.py:106
  141.6 10.2 %multiply_convert_fusion = (bf16[1024,768]{1,0:T(8,128)(2,1)}, bf16[1024,768]{1,0:T(8,128)(2,1)}, bf16[1024,768]{1,0:T(8,128)(2,1)S(1)}) fusion(f32[1024,768]{1,0:T(8,128)} %fusion.13, f32[1024,768]{1,0:T(8,128)} %fusion.11, bf16[1,768,2048]{2,1,0:T(8,128)(2,1)S(1)} %copy-done, bf16[128,8,2048]{2,1,0:T(8,128)(2,1)} %all-to-all-done.2), kind=kOutput, calls=%fused_computation.36 | convolution fusion | flops 3233808384 | bytes 18350080 | tf_op jit(solution)/shard_map/dot_general | solution.py:18
  151.7 1.1 copy-done.9
  152.8 5.0 %convert_bitcast_fusion = bf16[128,8,2048]{2,1,0:T(8,128)(2,1)} fusion(bf16[1024,768]{1,0:T(8,128)(2,1)S(1)} %get-tuple-element.8, bf16[1,768,2048]{2,1,0:T(8,128)(2,1)S(1)} %copy-done), kind=kOutput, calls=%fused_computation.25 | convolution fusion | flops 3223322624 | bytes 8912896 | tf_op jit(solution)/shard_map/dot_general | solution.py:11
  157.8 5.4 %all-to-all-start.1 = ((bf16[128,8,2048]{2,1,0:T(8,128)(2,1)}), bf16[128,8,2048]{2,1,0:T(8,128)(2,1)}, u32[]{:S(2)}, u32[]{:S(2)}) async-start(bf16[128,8,2048]{2,1,0:T(8,128)(2,1)} %convert_bitcast_fusion), calls=%async_computation.1 | async-start | bytes 8388608 | tf_op jit(solution)/shard_map/all_to_all | solution.py:99
  163.3 5.0 %fusion.28 = f32[1024,2048]{1,0:T(8,128)S(1)} fusion(bf16[1024,768]{1,0:T(8,128)(2,1)} %get-tuple-element.7, bf16[1,2048,768]{2,1,0:T(8,128)(2,1)S(1)} %copy-done.7), kind=kOutput, calls=%fused_computation.33 | convolution fusion | flops 3221225472 | bytes 13107200 | tf_op jit(solution)/shard_map/dot_general | solution.py:35
  168.3 5.0 %fusion.2 = bf16[128,8,2048]{2,1,0:T(8,128)(2,1)} fusion(f32[1024,2048]{1,0:T(8,128)S(1)} %fusion.28, bf16[1024,768]{1,0:T(8,128)(2,1)S(1)} %copy-done.12, bf16[1,2048,768]{2,1,0:T(8,128)(2,1)S(1)} %copy-done.8), kind=kOutput, calls=%fused_computation.11 | convolution fusion | flops 3225419776 | bytes 17301504 | tf_op jit(solution)/shard_map/dot_general | solution.py:38
  173.4 41.9 %all-to-all-done.1 = bf16[128,8,2048]{2,1,0:T(8,128)(2,1)} async-done(((bf16[128,8,2048]{2,1,0:T(8,128)(2,1)}), bf16[128,8,2048]{2,1,0:T(8,128)(2,1)}, u32[]{:S(2)}, u32[]{:S(2)}) %all-to-all-start.1) | async-done | bytes 4194336 | tf_op jit(solution)/shard_map/all_to_all | solution.py:99
  215.3 5.5 %all-to-all-start.3 = ((bf16[128,8,2048]{2,1,0:T(8,128)(2,1)}), bf16[128,8,2048]{2,1,0:T(8,128)(2,1)}, u32[]{:S(2)}, u32[]{:S(2)}) async-start(bf16[128,8,2048]{2,1,0:T(8,128)(2,1)} %fusion.2), calls=%async_computation.3 | async-start | bytes 8388608 | tf_op jit(solution)/shard_map/all_to_all | solution.py:113
  220.9 7.1 %fusion.31 = bf16[1,768,2048]{2,1,0:T(8,128)(2,1)} fusion(bf16[1024,768]{1,0:T(8,128)(2,1)S(1)} %copy-done.10, bf16[128,8,2048]{2,1,0:T(8,128)(2,1)} %all-to-all-done.2), kind=kOutput, calls=%fused_computation.40 | convolution fusion | flops 3222798336 | bytes 8912896 | tf_op jit(solution)/shard_map/dot_general | solution.py:26
  228.1 7.5 %fusion.34 = bf16[1,2048,768]{2,1,0:T(8,128)(2,1)} fusion(bf16[1024,768]{1,0:T(8,128)(2,1)S(1)} %copy-done.13, bf16[128,8,2048]{2,1,0:T(8,128)(2,1)} %all-to-all-done), kind=kOutput, calls=%fused_computation.41 | convolution fusion | flops 3222798336 | bytes 8912896 | tf_op jit(solution)/shard_map/dot_general | solution.py:32
  235.6 7.4 %fusion.37 = bf16[1,2048,768]{2,1,0:T(8,128)(2,1)} fusion(bf16[1024,768]{1,0:T(8,128)(2,1)S(1)} %copy-done.11, bf16[128,8,2048]{2,1,0:T(8,128)(2,1)} %all-to-all-done), kind=kOutput, calls=%fused_computation.42 | convolution fusion | flops 3222798336 | bytes 8912896 | tf_op jit(solution)/shard_map/dot_general | solution.py:29
  243.0 7.3 %gather_fusion.1 = bf16[512,2048]{1,0:T(8,128)(2,1)S(1)} fusion(bf16[1024,2048]{1,0:T(8,128)(2,1)} %bitcast.11, s32[1024]{0:T(1024)S(1)} %pad_clamp_fusion), kind=kCustom, calls=%fused_computation.1 | custom fusion | bytes 4196352 | tf_op jit(solution)/shard_map/gather | solution.py:120
  250.3 1.8 fusion.42
  253.0 1.4 fusion.40
  255.1 17.5 %all-to-all-done.3 = bf16[128,8,2048]{2,1,0:T(8,128)(2,1)} async-done(((bf16[128,8,2048]{2,1,0:T(8,128)(2,1)}), bf16[128,8,2048]{2,1,0:T(8,128)(2,1)}, u32[]{:S(2)}, u32[]{:S(2)}) %all-to-all-start.3) | async-done | bytes 4194336 | tf_op jit(solution)/shard_map/all_to_all | solution.py:113
  272.6 8.2 %gather_fusion.4 = bf16[512,2048]{1,0:T(8,128)(2,1)} fusion(bf16[1024,2048]{1,0:T(8,128)(2,1)} %bitcast.18, s32[1024]{0:T(1024)S(1)} %pad_clamp_fusion), kind=kCustom, calls=%fused_computation.4 | custom fusion | bytes 4196352 | tf_op jit(solution)/shard_map/gather | solution.py:123
  280.8 3.7 %bitcast_reduce_fusion = bf16[64,2048]{1,0:T(8,128)(2,1)} fusion(bf16[512,2048]{1,0:T(8,128)(2,1)} %gather_fusion.4), kind=kLoop, calls=%fused_computation.43 | loop fusion | flops 917504 | bytes 2359296 | tf_op jit(solution)/shard_map/reduce_sum | solution.py:52
  (53 shorter events, 4.6 us)
Async XLA Ops:
  0.6 140.9 %copy-start = (bf16[1,768,2048]{2,1,0:T(8,128)(2,1)S(1)}, bf16[1,768,2048]{2,1,0:T(8,128)(2,1)}, u32[]{:S(2)}) copy-start(bf16[1,768,2048]{2,1,0:T(8,128)(2,1)} %param.13) | copy-start | bytes 9437188
  0.6 9.5 %copy-start.2 = (bf16[64,2048]{1,0:T(8,128)(2,1)S(1)}, bf16[64,2048]{1,0:T(8,128)(2,1)}, u32[]{:S(2)}) copy-start(bf16[64,2048]{1,0:T(8,128)(2,1)} %param.7) | copy-start | bytes 786436
  3.1 0.7 copy-start.4
  20.7 11.3 %copy-start.5 = (f32[64,8]{0,1:T(8,128)S(1)}, f32[64,8]{0,1:T(8,128)}, u32[]{:S(2)}) copy-start(f32[64,8]{0,1:T(8,128)} %param.9) | copy-start | bytes 6148
  20.7 63.2 %all-to-all-start = ((bf16[128,8,2048]{2,1,0:T(8,128)(2,1)}), bf16[128,8,2048]{2,1,0:T(8,128)(2,1)}, u32[]{:S(2)}, u32[]{:S(2)}) async-start(bf16[128,8,2048]{2,1,0:T(8,128)(2,1)} %bitcast_select_fusion), calls=%async_computation | async-start | bytes 8388608 | tf_op jit(solution)/shard_map/all_to_all | solution.py:96
  32.0 7.2 %copy-start.3 = (bf16[64,2048]{1,0:T(8,128)(2,1)S(1)}, bf16[64,2048]{1,0:T(8,128)(2,1)}, u32[]{:S(2)}) copy-start(bf16[64,2048]{1,0:T(8,128)(2,1)} %param.10) | copy-start | bytes 786436
  83.9 57.6 %all-to-all-start.2 = ((bf16[128,8,2048]{2,1,0:T(8,128)(2,1)}), bf16[128,8,2048]{2,1,0:T(8,128)(2,1)}, u32[]{:S(2)}, u32[]{:S(2)}) async-start(bf16[128,8,2048]{2,1,0:T(8,128)(2,1)} %fusion.1), calls=%async_computation.2 | async-start | bytes 8388608 | tf_op jit(solution)/shard_map/all_to_all | solution.py:106
  89.7 8.4 %copy-start.6 = (bf16[1,2048,768]{2,1,0:T(8,128)(2,1)S(1)}, bf16[1,2048,768]{2,1,0:T(8,128)(2,1)}, u32[]{:S(2)}) copy-start(bf16[1,2048,768]{2,1,0:T(8,128)(2,1)} %param.11) | copy-start | bytes 9437188
  151.7 1.1 copy-start.9
  157.8 5.4 %copy-start.7 = (bf16[1,2048,768]{2,1,0:T(8,128)(2,1)S(1)}, bf16[1,2048,768]{2,1,0:T(8,128)(2,1)}, u32[]{:S(2)}) copy-start(bf16[1,2048,768]{2,1,0:T(8,128)(2,1)} %param.11) | copy-start | bytes 9437188
  157.8 57.5 %all-to-all-start.1 = ((bf16[128,8,2048]{2,1,0:T(8,128)(2,1)}), bf16[128,8,2048]{2,1,0:T(8,128)(2,1)}, u32[]{:S(2)}, u32[]{:S(2)}) async-start(bf16[128,8,2048]{2,1,0:T(8,128)(2,1)} %convert_bitcast_fusion), calls=%async_computation.1 | async-start | bytes 8388608 | tf_op jit(solution)/shard_map/all_to_all | solution.py:99
  163.3 5.0 %copy-start.8 = (bf16[1,2048,768]{2,1,0:T(8,128)(2,1)S(1)}, bf16[1,2048,768]{2,1,0:T(8,128)(2,1)}, u32[]{:S(2)}) copy-start(bf16[1,2048,768]{2,1,0:T(8,128)(2,1)} %param.12) | copy-start | bytes 9437188
  163.3 5.0 %copy-start.12 = (bf16[1024,768]{1,0:T(8,128)(2,1)S(1)}, bf16[1024,768]{1,0:T(8,128)(2,1)}, u32[]{:S(2)}) copy-start(bf16[1024,768]{1,0:T(8,128)(2,1)} %get-tuple-element.6) | copy-start | bytes 4718596
  173.4 47.6 %copy-start.10 = (bf16[1024,768]{1,0:T(8,128)(2,1)S(1)}, bf16[1024,768]{1,0:T(8,128)(2,1)}, u32[]{:S(2)}) copy-start(bf16[1024,768]{1,0:T(8,128)(2,1)} %copy-done.9) | copy-start | bytes 4718596
  215.3 57.3 %all-to-all-start.3 = ((bf16[128,8,2048]{2,1,0:T(8,128)(2,1)}), bf16[128,8,2048]{2,1,0:T(8,128)(2,1)}, u32[]{:S(2)}, u32[]{:S(2)}) async-start(bf16[128,8,2048]{2,1,0:T(8,128)(2,1)} %fusion.2), calls=%async_computation.3 | async-start | bytes 8388608 | tf_op jit(solution)/shard_map/all_to_all | solution.py:113
  220.9 7.2 %copy-start.13 = (bf16[1024,768]{1,0:T(8,128)(2,1)S(1)}, bf16[1024,768]{1,0:T(8,128)(2,1)}, u32[]{:S(2)}) copy-start(bf16[1024,768]{1,0:T(8,128)(2,1)} %get-tuple-element.6) | copy-start | bytes 4718596
  228.1 7.5 %copy-start.11 = (bf16[1024,768]{1,0:T(8,128)(2,1)S(1)}, bf16[1024,768]{1,0:T(8,128)(2,1)}, u32[]{:S(2)}) copy-start(bf16[1024,768]{1,0:T(8,128)(2,1)} %get-tuple-element.7) | copy-start | bytes 4718596
  272.6 11.9 %copy-start.1 = (bf16[1,768,2048]{2,1,0:T(8,128)(2,1)S(1)}, bf16[1,768,2048]{2,1,0:T(8,128)(2,1)}, u32[]{:S(2)}) copy-start(bf16[1,768,2048]{2,1,0:T(8,128)(2,1)} %param.13) | copy-start | bytes 9437188
where the time goes:
time: 290 us; the launch traced here: 285 us
  waiting for transfers between devices  130 us (45%)
  matrix products  66.1 us (23%)
  local copies, waits for them, and re-layouts  44.6 us (15%)
  starting transfers between devices  28 us (10%)
  other arithmetic  14.7 us (5%)
    all_to_all x1, waiting for transfers between devices, per_device(): lax.all_to_all(output.reshape(experts, capacity, model_width), ('node', '...  41.9 us
    all_to_all x1, waiting for transfers between devices, per_device(): lax.all_to_all(send_grads, ('node', 'rail'), split_axis=0, concat_axis=0,...  36.1 us
    all_to_all x1, waiting for transfers between devices, per_device(): lax.all_to_all(send_rows, ('node', 'rail'), split_axis=0, concat_axis=0,...  34.6 us
    all_to_all x1, waiting for transfers between devices, per_device(): lax.all_to_all(input_back.reshape(experts, capacity, model_width), ('node...  17.5 us
    all_to_all x1, starting transfers between devices, per_device(): lax.all_to_all(send_rows, ('node', 'rail'), split_axis=0, concat_axis=0,...  11.2 us
    dot_general x1, matrix products, expert_backward(): lax.dot_general(slot_grads, w_down, contract_last, preferred_element_type...  10.2 us
    dot_general x1, matrix products, expert_forward(): up_pre = jnp.dot(slot_rows, w_up, preferred_element_type=jnp.float32)  8.37 us
    gather x1, local copies, waits for them, and re-layouts, per_device(): back_home.reshape(-1, model_width)[slot_index]  8.16 us
  transfers between devices with their start and end apart: 4, of which 4 were waited for; matrix products, arithmetic and copies ran while one was open for 27% of the time, Pallas kernels for 0%

commit v1 on v0

--- a/solution.py
+++ b/solution.py
@@ -1,7 +1,268 @@
 import jax
 import jax.numpy as jnp
 from jax import lax
+from jax.experimental import pallas as pl
+from jax.experimental.pallas import tpu as pltpu
 from jax.sharding import PartitionSpec as P
+
+MESH = pl.DeviceIdType.MESH
+F32, BF16 = jnp.float32, jnp.bfloat16
+PARTS = ((0, 1, 2, 0, 768), (1, 2, 0, 768, 640), (2, 0, 1, 1408, 640))
+
+
+def place():
+    node, rail = lax.axis_index("node"), lax.axis_index("rail")
+    return (node // 2, rail % 4, rail // 4), node % 2
+
+
+def moved(co, axis, value):
+    return tuple(value if i == axis else v for i, v in enumerate(co))
+
+
+def device(co, core):
+    return (co[0] * 2 + core, co[2] * 4 + co[1])
+
+
+def remote(src, dst, send, recv, target):
+    return pltpu.make_async_remote_copy(
+        src_ref=src, dst_ref=dst, send_sem=send, recv_sem=recv, device_id=target, device_id_type=MESH
+    )
+
+
+def greet(co, core):
+    barrier = pltpu.get_barrier_semaphore()
+    targets = [device(co, 1 - core)]
+    for axis in range(3):
+        for step in (1, 2, 3):
+            there = moved(co, axis, (co[axis] + step) % 4)
+            targets += [device(there, core), device(there, 1 - core)]
+    for target in targets:
+        pl.semaphore_signal(barrier, inc=1, device_id=target, device_id_type=MESH)
+    return barrier, len(targets)
+
+
+def route_tables(routes, weights):
+    lanes = lax.broadcasted_iota(jnp.int32, (64, 128), 1)
+    named = jnp.zeros((64, 128), F32)
+    for k in range(8):
+        named = named + jnp.where(routes[:, k : k + 1] == lanes, 1.0, 0.0)
+    row = lax.broadcasted_iota(jnp.int32, (64, 64), 0)
+    col = lax.broadcasted_iota(jnp.int32, (64, 64), 1)
+    upto = jnp.where(col <= row, 1.0, 0.0).astype(BF16)
+    counted = jnp.dot(upto, named.astype(BF16), preferred_element_type=F32)
+    table = (counted * named).astype(BF16)
+    extra = jnp.zeros((64, 128), F32)
+    for k in range(8):
+        w = weights[:, k : k + 1]
+        high = w.astype(BF16).astype(F32)
+        mid = (w - high).astype(BF16).astype(F32)
+        low = w - high - mid
+        extra = jnp.where(lanes == k, (routes[:, k : k + 1] + 1).astype(F32), extra)
+        extra = jnp.where(lanes == 8 + k, high, extra)
+        extra = jnp.where(lanes == 16 + k, mid, extra)
+        extra = jnp.where(lanes == 24 + k, low, extra)
+    return table, extra.astype(BF16)
+
+
+def one_hot(table, co, slot_axis):
+    expert = lax.broadcasted_iota(jnp.int32, (128, 256), 0)
+    lane = lax.broadcasted_iota(jnp.int32, (128, 256), 1)
+    core, along = lane // 128, (lane // 32) % 4
+    there = moved(co, slot_axis, along)
+    owner = (there[0] * 2 + core) * 16 + there[2] * 4 + there[1]
+    spread = jnp.dot(table, jnp.where(expert == owner, 1.0, 0.0).astype(BF16), preferred_element_type=F32)
+    row = lax.broadcasted_iota(jnp.int32, (256, 256), 0)
+    lane = lax.broadcasted_iota(jnp.int32, (256, 256), 1)
+    wanted = jnp.where(row // 64 == (lane // 8) % 4, lane % 8 + 1, -1).astype(F32)
+    return jnp.where(spread == wanted, 1.0, 0.0).astype(BF16)
+
+
+def dispatch_kernel(tok, cot, routes, weights, *refs):
+    xo, co_, rwo, st = refs[0:3], refs[3:6], refs[6], refs[7]
+    xb, cb, qb, rwb = refs[8:11], refs[11:14], refs[14:17], refs[17]
+    xs, cs, rws = refs[18:21], refs[21:24], refs[24]
+    s1, r1, s2, r2, s3, r3, loc = refs[25:32]
+    co, core = place()
+    barrier, count = greet(co, core)
+    table, extra = route_tables(routes[...], weights[...])
+    for p, (a1, a2, _, c0, cols) in enumerate(PARTS):
+        xb[p][co[a2], co[a1]] = tok[:, c0 : c0 + cols]
+        cb[p][co[a2], co[a1]] = cot[:, c0 : c0 + cols]
+        qb[p][co[a2], co[a1]] = table
+    rwb[co[1], co[0]] = extra
+    pl.semaphore_wait(barrier, count)
+
+    tables = [(qb[p], p, p) for p in range(3)] + [(rwb, 0, 3)]
+    rows = [(xb[p], p, 4 + p) for p in range(3)]
+    grads = [(cb[p], p, 7 + p) for p in range(3)]
+
+    def first_copies(buf, p, n):
+        a1, a2 = PARTS[p][:2]
+        mine = buf.at[co[a2], co[a1]]
+        return [
+            remote(mine, mine, s1.at[n, d - 1], r1.at[n, co[a1]], device(moved(co, a1, (co[a1] + d) % 4), core))
+            for d in (1, 2, 3)
+        ]
+
+    def first_wait(buf, p, n):
+        a1, a2 = PARTS[p][:2]
+        for d in (1, 2, 3):
+            i = (co[a1] + d) % 4
+            got = buf.at[co[a2], i]
+            remote(got, got, s1.at[n, d - 1], r1.at[n, i], device(moved(co, a1, i), core)).wait_recv()
+
+    def half(buf, block, h):
+        return buf.at[block, pl.ds(2 * h, 2)]
+
+    def second_copy(buf, p, n, block, h, right, number):
+        a2 = PARTS[p][1]
+        part = half(buf, block, h)
+        target = device(moved(co, a2, (co[a2] + (1 if right else 3)) % 4), core)
+        return remote(part, part, s2.at[n, number], r2.at[n, block, h], target)
+
+    def second_first(buf, p, n):
+        me = co[PARTS[p][1]]
+        return [
+            second_copy(buf, p, n, me, 0, True, 0),
+            second_copy(buf, p, n, me, 1, False, 1),
+            second_copy(buf, p, n, me, 1, True, 2),
+            second_copy(buf, p, n, me, 0, False, 3),
+        ]
+
+    def second_wait(buf, p, n, d, h):
+        a2 = PARTS[p][1]
+        block = (co[a2] + d) % 4
+        second_copy(buf, p, n, block, h, True, 0).wait_recv()
+
+    def relay(buf, p, n):
+        a2 = PARTS[p][1]
+        second_wait(buf, p, n, 3, 0)
+        a = second_copy(buf, p, n, (co[a2] + 3) % 4, 0, True, 4)
+        a.start()
+        second_wait(buf, p, n, 1, 1)
+        b = second_copy(buf, p, n, (co[a2] + 1) % 4, 1, False, 5)
+        b.start()
+        return [a, b]
+
+    def rest_wait(buf, p, n):
+        second_wait(buf, p, n, 3, 1)
+        second_wait(buf, p, n, 1, 0)
+        second_wait(buf, p, n, 2, 0)
+        second_wait(buf, p, n, 2, 1)
+
+    sent = []
+
+    def start(copies):
+        for c in copies:
+            c.start()
+        sent.extend(copies)
+
+    for item in tables + rows + grads:
+        start(first_copies(*item))
+    for item in tables + rows:
+        first_wait(*item)
+        start(second_first(*item))
+    for item in grads:
+        first_wait(*item)
+        start(second_first(*item))
+    for item in tables + rows:
+        sent.extend(relay(*item))
+    for item in tables:
+        rest_wait(*item)
+    for p, (_, _, slot_axis, _, _) in enumerate(PARTS):
+
+        def build(g, _, p=p, slot_axis=slot_axis):
+            st[p, g] = one_hot(qb[p][g].reshape(256, 128), co, slot_axis)
+            return 0
+
+        lax.fori_loop(0, 4, build, 0)
+
+    def pick(buf, out, p):
+        cols = buf.shape[-1]
+
+        def step(g, _):
+            r = lax.dot_general(
+                st[p, g], buf[g].reshape(256, cols), (((0,), (0,)), ((), ())), preferred_element_type=F32
+            )
+            out[:, pl.ds(pl.multiple_of(g * 32, 32), 32), :] = r.astype(BF16).reshape(8, 32, cols)
+            return 0
+
+        lax.fori_loop(0, 4, step, 0)
+
+    def slot_copies(src, dst, p, n):
+        axis = PARTS[p][2]
+        me = core * 4 + co[axis]
+        remotes = []
+        for dc in (0, 1):
+            for d in (1, 3, 2, 0):
+                if dc == 0 and d == 0:
+                    continue
+                there, other = (co[axis] + d) % 4, (core + dc) % 2
+                k = other * 4 + there
+                remotes.append(
+                    remote(src.at[k], dst.at[me], s3.at[n, dc * 4 + d], r3.at[n, me], device(moved(co, axis, there), other))
+                )
+        return remotes, pltpu.make_async_copy(src.at[me], dst.at[me], loc.at[n])
+
+    def slot_wait(src, dst, p, n):
+        axis = PARTS[p][2]
+        for dc in (0, 1):
+            for d in (1, 3, 2, 0):
+                if dc == 0 and d == 0:
+                    continue
+                there, other = (co[axis] + d) % 4, (core + dc) % 2
+                k = other * 4 + there
+                remote(src.at[k], dst.at[k], s3.at[n, dc * 4 + d], r3.at[n, k], device(moved(co, axis, there), other)).wait_recv()
+
+    slots = []
+
+    def send(src, dst, p, n):
+        remotes, local = slot_copies(src, dst, p, n)
+        start(remotes)
+        local.start()
+        slots.append((src, dst, p, n, local))
+
+    pick(rwb, rws, 0)
+    send(rws, rwo, 0, 0)
+    for p in range(3):
+        rest_wait(*rows[p])
+        pick(xb[p], xs[p], p)
+        send(xs[p], xo[p], p, 1 + p)
+    for item in grads:
+        sent.extend(relay(*item))
+    for p in range(3):
+        rest_wait(*grads[p])
+        pick(cb[p], cs[p], p)
+        send(cs[p], co_[p], p, 4 + p)
+    for src, dst, p, n, local in slots:
+        slot_wait(src, dst, p, n)
+        local.wait()
+    for c in sent:
+        c.wait_send()
+
+
+def dispatch(tokens, cotangent, routes, weights):
+    widths = [part[4] for part in PARTS]
+    outs = (
+        [jax.ShapeDtypeStruct((8, 128, w), BF16) for w in widths] * 2
+        + [jax.ShapeDtypeStruct((8, 128, 128), BF16), jax.ShapeDtypeStruct((3, 4, 256, 256), BF16)]
+    )
+    any_, vmem = pl.BlockSpec(memory_space=pl.ANY), pl.BlockSpec(memory_space=pltpu.VMEM)
+    gathered = [pltpu.VMEM((4, 4, 64, w), BF16) for w in widths]
+    table = pltpu.VMEM((4, 4, 64, 128), BF16)
+    sends = [pltpu.VMEM((8, 128, w), BF16) for w in widths]
+    dma = pltpu.SemaphoreType.DMA
+    return pl.pallas_call(
+        dispatch_kernel,
+        out_shape=outs,
+        in_specs=[vmem] * 4,
+        out_specs=[any_] * 7 + [vmem],
+        scratch_shapes=gathered * 2 + [table] * 4 + sends * 2 + [pltpu.VMEM((8, 128, 128), BF16)]
+        + [dma((10, 3)), dma((10, 4)), dma((10, 6)), dma((10, 4, 2)), dma((7, 8)), dma((7, 8)), dma((7,))],
+        compiler_params=pltpu.CompilerParams(
+            collective_id=0, has_side_effects=True, vmem_limit_bytes=56 * 2**20
+        ),
+    )(tokens, cotangent, routes, weights)
 
 
 def expert_forward(slot_rows, w_gate, w_up, w_down):
@@ -53,76 +314,45 @@
     return (mixed, token_grad, weight_grad)
 
 
+def canonical(parts):
+    a, b, c = parts
+    w = [part[4] for part in PARTS]
+    a = a.reshape(2, 4, 4, 4, 8, w[0]).transpose(3, 0, 1, 2, 4, 5)
+    b = b.reshape(2, 4, 4, 4, 8, w[1]).transpose(1, 0, 2, 3, 4, 5)
+    c = c.reshape(2, 4, 4, 4, 8, w[2]).transpose(2, 0, 3, 1, 4, 5)
+    return jnp.concatenate([a, b, c], axis=-1).reshape(1024, 2048)
+
+
 def per_device(tokens, routes, route_weights, cotangent, gate_weight, up_weight, down_weight):
+    out = dispatch(tokens, cotangent, routes, route_weights)
+    slot_rows, slot_cots = canonical(out[0:3]), canonical(out[3:6])
+    extra = out[6].reshape(2, 4, 4, 4, 8, 128).transpose(3, 0, 1, 2, 4, 5).reshape(1024, 128).astype(jnp.float32)
+    own = lax.axis_index(("node", "rail")) + 1
+    weight = jnp.sum(
+        jnp.where(extra[:, :8] == own.astype(jnp.float32), extra[:, 8:16] + extra[:, 16:24] + extra[:, 24:32], 0.0), axis=1
+    )
+    slot_grads = (weight[:, None] * slot_cots.astype(jnp.float32)).astype(jnp.bfloat16)
     token_count, model_width = tokens.shape
     top_count = routes.shape[1]
-    experts = lax.axis_size(("node", "rail"))
-    capacity = 2 * token_count * top_count // experts
+    experts, capacity = 128, 8
     flat_routes = routes.reshape(-1)
-    onehot = (flat_routes[:, None] == jnp.arange(experts, dtype=jnp.int32)[None, :]).astype(
-        jnp.int32
-    )
+    onehot = (flat_routes[:, None] == jnp.arange(experts, dtype=jnp.int32)[None, :]).astype(jnp.int32)
     position = jnp.sum((jnp.cumsum(onehot, axis=0) - onehot) * onehot, axis=1)
     slot_index = flat_routes * capacity + position
-    total_slots = experts * capacity
-    owner_row = (
-        jnp.zeros((total_slots,), jnp.int32)
-        .at[slot_index]
-        .set(jnp.arange(token_count * top_count, dtype=jnp.int32))
-    )
-    filled = (
-        jnp.zeros((total_slots,), jnp.int32)
-        .at[slot_index]
-        .set(jnp.ones((token_count * top_count,), jnp.int32))
-    )
-    token_of = owner_row // top_count
-    weight_of = route_weights.reshape(-1)[owner_row]
-    keep_mask = (filled > 0)[:, None]
-    send_rows = jnp.where(keep_mask, tokens[token_of], jnp.zeros((), jnp.bfloat16)).reshape(
-        experts, capacity, model_width
-    )
-    send_grads = (
-        jnp.where(
-            keep_mask,
-            weight_of[:, None] * cotangent[token_of].astype(jnp.float32),
-            jnp.float32(0.0),
-        )
-        .astype(jnp.bfloat16)
-        .reshape(experts, capacity, model_width)
-    )
-    w_gate = gate_weight[0]
-    w_up = up_weight[0]
-    w_down = down_weight[0]
-    recv_rows = lax.all_to_all(send_rows, ("node", "rail"), split_axis=0, concat_axis=0, tiled=True)
-    slot_rows = recv_rows.reshape(-1, model_width)
+    w_gate, w_up, w_down = gate_weight[0], up_weight[0], down_weight[0]
     gate_pre, up_pre, hidden, output = expert_forward(slot_rows, w_gate, w_up, w_down)
+    names = ("node", "rail")
     out_home = lax.all_to_all(
-        output.reshape(experts, capacity, model_width),
-        ("node", "rail"),
-        split_axis=0,
-        concat_axis=0,
-        tiled=True,
-    )
-    recv_grads = lax.all_to_all(
-        send_grads, ("node", "rail"), split_axis=0, concat_axis=0, tiled=True
-    )
-    slot_grads = recv_grads.reshape(-1, model_width)
+        output.reshape(experts, capacity, model_width), names, split_axis=0, concat_axis=0, tiled=True
+    )
     input_back, gate_grad, up_grad, down_grad = expert_backward(
         slot_rows, slot_grads, gate_pre, up_pre, hidden, w_gate, w_up, w_down
     )
     back_home = lax.all_to_all(
-        input_back.reshape(experts, capacity, model_width),
-        ("node", "rail"),
-        split_axis=0,
-        concat_axis=0,
-        tiled=True,
-    )
-    out_slot = out_home.reshape(-1, model_width)[slot_index].reshape(
-        token_count, top_count, model_width
-    )
-    back_slot = back_home.reshape(-1, model_width)[slot_index].reshape(
-        token_count, top_count, model_width
-    )
+        input_back.reshape(experts, capacity, model_width), names, split_axis=0, concat_axis=0, tiled=True
+    )
+    out_slot = out_home.reshape(-1, model_width)[slot_index].reshape(token_count, top_count, model_width)
+    back_slot = back_home.reshape(-1, model_width)[slot_index].reshape(token_count, top_count, model_width)
     mixed, token_grad, weight_grad = combine_slots(out_slot, back_slot, route_weights, cotangent)
     return (mixed, token_grad, weight_grad, gate_grad[None], up_grad[None], down_grad[None])
 

time: 290 us -> 252 us (0.87); the launches traced: 285 us -> 252 us
  Pallas kernels: 0 us -> 90.8 us
  waiting for transfers between devices: 130 us -> 62.3 us
  matrix products: 66.1 us -> 46.9 us
  starting transfers between devices: 28 us -> 11.9 us
  local copies, waits for them, and re-layouts: 44.6 us -> 31.3 us
  other arithmetic: 14.7 us -> 7.29 us
    pallas_call x0 -> x1, Pallas kernels: none -> 90.8 us  [dispatch(): pl.pallas_call(dispatch_kernel, out_shape=outs, in_specs=[vmem] * 4, out_...]
    all_to_all x4 -> x2, waiting for transfers between devices: 130 us -> 62.3 us  [the longest x1 40.6 us: per_device(): lax.all_to_all(output.reshape(experts, capacity, model_width), names, spl...]
    gather x3 -> x0, local copies, waits for them, and re-layouts: 18.9 us -> none  [the longest x1 6.86 us: per_device(): weight_of = route_weights.reshape(-1)[owner_row]]
    all_to_all x4 -> x2, starting transfers between devices: 28 us -> 11.9 us  [the longest x1 6.7 us: per_device(): lax.all_to_all(output.reshape(experts, capacity, model_width), names, spl...]
    unnamed x32 -> x60, local copies, waits for them, and re-layouts: 3 us -> 11.3 us
    dot_general x1, matrix products: 8.37 us -> 3.4 us  [expert_forward(): up_pre = jnp.dot(slot_rows, w_up, preferred_element_type=jnp.float32)]
    scatter x2 -> x0, local copies, waits for them, and re-layouts: 4.89 us -> none  [the longest x1 2.45 us: per_device(): owner_row = jnp.zeros((total_slots,), jnp.int32).at[slot_index].set(jnp.a...]
    select_n x2 -> x1, other arithmetic: 4.54 us -> 0.01 us  [per_device(): out_home.reshape(-1, model_width)[slot_index]]
  transfers between devices with their start and end apart: 4 -> 2, of which waited for: 4 -> 2; matrix products, arithmetic and copies ran while one was open for 27% -> 16% of each run, Pallas kernels for 0% -> 0%
where the time goes in v1:
time: 252 us
  Pallas kernels  90.8 us (36%)
  waiting for transfers between devices  62.3 us (25%)
  matrix products  46.9 us (19%)
  local copies, waits for them, and re-layouts  31.3 us (12%)
  starting transfers between devices  11.9 us (5%)
  other arithmetic  7.29 us (3%)
    pallas_call x1, Pallas kernels, dispatch(): pl.pallas_call(dispatch_kernel, out_shape=outs, in_specs=[vmem] * 4, out_...  90.8 us
    all_to_all x1, waiting for transfers between devices, per_device(): lax.all_to_all(output.reshape(experts, capacity, model_width), names, spl...  40.6 us
    all_to_all x1, waiting for transfers between devices, per_device(): lax.all_to_all(input_back.reshape(experts, capacity, model_width), names,...  21.7 us
    unnamed x60, local copies, waits for them, and re-layouts  11.3 us
    gather x1, local copies, waits for them, and re-layouts, per_device(): back_home.reshape(-1, model_width)[slot_index]  8.34 us
    gather x1, local copies, waits for them, and re-layouts, per_device(): out_home.reshape(-1, model_width)[slot_index]  7.13 us
    all_to_all x1, starting transfers between devices, per_device(): lax.all_to_all(output.reshape(experts, capacity, model_width), names, spl...  6.7 us
    dot_general x1, matrix products, expert_backward(): lax.dot_general(slot_grads, w_down, contract_last, preferred_element_type...  6.5 us
  transfers between devices with their start and end apart: 2, of which 2 were waited for; matrix products, arithmetic and copies ran while one was open for 16% of the time, Pallas kernels for 0%

profile of v1, /device:TPU:7, one launch (start us, length us, event | category | flops | bytes accessed | tf_op | source)
XLA Modules:
  0.0 251.6 jit_solution(17455780337222035929)
XLA Ops:
  0.7 1.5 copy.19.routes
  2.2 1.4 copy.20.weights
  3.6 90.8 %shard_map.118 = (bf16[8,128,768]{2,1,0:T(8,128)(2,1)}, bf16[8,128,640]{2,1,0:T(8,128)(2,1)}, bf16[8,128,640]{2,1,0:T(8,128)(2,1)}, bf16[8,128,768]{2,1,0:T(8,12...) custom-call(bf16[64,2048]{1,0:T(8,128)(2,1)} %tok.1, ...), custom_call_target="tpu_custom_call" | custom-call | tf_op jit(solution)/shard_map/pallas_call | solution.py:255
  94.4 1.7 copy.49
  96.9 0.8 copy-done.11
  98.5 0.8 copy-done.9
  99.5 0.6 pad_maximum_fusion
  100.2 3.3 %copy-done.20 = bf16[1,2048,768]{2,1,0:T(8,128)(2,1)S(1)} copy-done((bf16[1,2048,768]{2,1,0:T(8,128)(2,1)S(1)}, bf16[1,2048,768]{2,1,0:T(8,128)(2,1)}, u32[]{:S(2)}) %copy-start.20) | copy-done | bytes 3145752
  103.5 3.4 %fusion.18 = f32[1024,768]{1,0:T(8,128)S(1)} fusion(bf16[1024,2048]{1,0:T(8,128)(2,1)S(1)} %bitcast.116, bf16[1,2048,768]{2,1,0:T(8,128)(2,1)S(1)} %copy-done.20), kind=kOutput, calls=%fused_computation.25 | convolution fusion | flops 3221225472 | bytes 10485760 | tf_op jit(solution)/shard_map/dot_general | solution.py:270
  106.9 3.4 %fusion.22 = f32[1024,768]{1,0:T(8,128)S(1)} fusion(bf16[1024,2048]{1,0:T(8,128)(2,1)S(1)} %bitcast.117, bf16[1,2048,768]{2,1,0:T(8,128)(2,1)S(1)} %copy-done.19), kind=kOutput, calls=%fused_computation.29 | convolution fusion | flops 3221225472 | bytes 10485760 | tf_op jit(solution)/shard_map/dot_general | solution.py:269
  110.4 0.6 fusion.34
  111.1 6.5 %multiply_convert_fusion.2 = (bf16[1024,768]{1,0:T(8,128)(2,1)}, bf16[1024,768]{1,0:T(8,128)(2,1)}, bf16[1024,768]{1,0:T(8,128)(2,1)S(1)}) fusion(f32[1024,768]{1,0:T(8,128)S(1)} %fusion.22, f32[1024,768]{1,0:T(8,128)S(1)} %fusion.18, bf16[1,768,2048]{2,1,0:T(8,128)(2,1)S(1)} %copy-done, bf16[1024,640]{1,0:T(8,128)(2,1)S(1)} %bitcast.112, ...), kind=kOutput, calls=%fused_computation.31 | convolution fusion | flops 3250585600 | bytes 18354176 | tf_op jit(solution)/shard_map/dot_general | solution.py:279
  117.6 1.2 copy-done.22
  118.7 5.0 %convert_bitcast_fusion = bf16[128,8,2048]{2,1,0:T(8,128)(2,1)} fusion(bf16[1024,768]{1,0:T(8,128)(2,1)S(1)} %get-tuple-element.22, bf16[1,768,2048]{2,1,0:T(8,128)(2,1)S(1)} %copy-done), kind=kOutput, calls=%fused_computation.18 | convolution fusion | flops 3223322624 | bytes 8912896 | tf_op jit(solution)/shard_map/dot_general | solution.py:272
  123.7 6.7 %all-to-all-start = ((bf16[128,8,2048]{2,1,0:T(8,128)(2,1)}), bf16[128,8,2048]{2,1,0:T(8,128)(2,1)}, u32[]{:S(2)}, u32[]{:S(2)}) async-start(bf16[128,8,2048]{2,1,0:T(8,128)(2,1)} %convert_bitcast_fusion), calls=%async_computation | async-start | bytes 8388608 | tf_op jit(solution)/shard_map/all_to_all | solution.py:345
  131.3 5.5 %fusion.20 = f32[1024,2048]{1,0:T(8,128)S(1)} fusion(bf16[1024,768]{1,0:T(8,128)(2,1)S(1)} %copy-done.24, bf16[1,2048,768]{2,1,0:T(8,128)(2,1)} %param.11), kind=kOutput, calls=%fused_computation.27 | convolution fusion | flops 3221225472 | bytes 13107200 | tf_op jit(solution)/shard_map/dot_general | solution.py:296
  136.8 5.0 %fusion.2 = bf16[128,8,2048]{2,1,0:T(8,128)(2,1)} fusion(f32[1024,2048]{1,0:T(8,128)S(1)} %fusion.20, bf16[1024,768]{1,0:T(8,128)(2,1)S(1)} %copy-done.26, bf16[1,2048,768]{2,1,0:T(8,128)(2,1)S(1)} %copy-done.21), kind=kOutput, calls=%fused_computation.7 | convolution fusion | flops 3225419776 | bytes 17301504 | tf_op jit(solution)/shard_map/dot_general | solution.py:299
  141.8 40.6 %all-to-all-done = bf16[128,8,2048]{2,1,0:T(8,128)(2,1)} async-done(((bf16[128,8,2048]{2,1,0:T(8,128)(2,1)}), bf16[128,8,2048]{2,1,0:T(8,128)(2,1)}, u32[]{:S(2)}, u32[]{:S(2)}) %all-to-all-start) | async-done | bytes 4194336 | tf_op jit(solution)/shard_map/all_to_all | solution.py:345
  182.4 5.2 %all-to-all-start.1 = ((bf16[128,8,2048]{2,1,0:T(8,128)(2,1)}), bf16[128,8,2048]{2,1,0:T(8,128)(2,1)}, u32[]{:S(2)}, u32[]{:S(2)}) async-start(bf16[128,8,2048]{2,1,0:T(8,128)(2,1)} %fusion.2), calls=%async_computation.1 | async-start | bytes 8388608 | tf_op jit(solution)/shard_map/all_to_all | solution.py:351
  188.0 1.8 pad_maximum_fusion.1
  189.8 0.8 copy-done.8
  191.0 4.9 %fusion.25 = bf16[1,2048,768]{2,1,0:T(8,128)(2,1)} fusion(bf16[1024,2048]{1,0:T(8,128)(2,1)S(1)} %bitcast.118, bf16[1024,768]{1,0:T(8,128)(2,1)S(1)} %copy-done.27), kind=kOutput, calls=%fused_computation.36 | convolution fusion | flops 3222798336 | bytes 8912896 | tf_op jit(solution)/shard_map/dot_general | solution.py:293
  195.9 4.9 %fusion.24 = bf16[1,2048,768]{2,1,0:T(8,128)(2,1)} fusion(bf16[1024,2048]{1,0:T(8,128)(2,1)S(1)} %bitcast.119, bf16[1024,768]{1,0:T(8,128)(2,1)S(1)} %copy-done.25), kind=kOutput, calls=%fused_computation.35 | convolution fusion | flops 3222798336 | bytes 8912896 | tf_op jit(solution)/shard_map/dot_general | solution.py:290
  200.8 5.1 %fusion.26 = bf16[1,768,2048]{2,1,0:T(8,128)(2,1)} fusion(bf16[1024,768]{1,0:T(8,128)(2,1)S(1)} %copy-done.23, bf16[1024,2048]{1,0:T(8,128)(2,1)S(1)} %bitcast.120, f32[1024]{0:T(1024)S(1)} %fusion.34), kind=kOutput, calls=%fused_computation.37 | convolution fusion | flops 3229089792 | bytes 8916992 | tf_op jit(solution)/shard_map/dot_general | solution.py:287
  205.9 7.1 %gather_fusion = bf16[512,2048]{1,0:T(8,128)(2,1)S(1)} fusion(bf16[1024,2048]{1,0:T(8,128)(2,1)} %bitcast.11, s32[1024]{0:T(1024)S(1)} %pad_clamp_fusion), kind=kCustom, calls=%fused_computation | custom fusion | bytes 4196352 | tf_op jit(solution)/shard_map/gather | solution.py:354
  213.0 1.8 fusion.31
  214.9 0.9 copy.52
  215.7 1.4 fusion.29
  217.1 0.7 copy.36
  217.8 21.7 %all-to-all-done.1 = bf16[128,8,2048]{2,1,0:T(8,128)(2,1)} async-done(((bf16[128,8,2048]{2,1,0:T(8,128)(2,1)}), bf16[128,8,2048]{2,1,0:T(8,128)(2,1)}, u32[]{:S(2)}, u32[]{:S(2)}) %all-to-all-start.1) | async-done | bytes 4194336 | tf_op jit(solution)/shard_map/all_to_all | solution.py:351
  239.5 8.3 %gather_fusion.1 = bf16[512,2048]{1,0:T(8,128)(2,1)} fusion(bf16[1024,2048]{1,0:T(8,128)(2,1)} %bitcast.34, s32[1024]{0:T(1024)S(1)} %pad_clamp_fusion), kind=kCustom, calls=%fused_computation.1 | custom fusion | bytes 4196352 | tf_op jit(solution)/shard_map/gather | solution.py:355
  247.8 3.7 %bitcast_reduce_fusion = bf16[64,2048]{1,0:T(8,128)(2,1)} fusion(bf16[512,2048]{1,0:T(8,128)(2,1)} %gather_fusion.1), kind=kLoop, calls=%fused_computation.38 | loop fusion | flops 917504 | bytes 2359296 | tf_op jit(solution)/shard_map/reduce_sum | solution.py:313
  (74 shorter events, 3.3 us)
Async XLA Ops:
  0.6 110.4 %copy-start = (bf16[1,768,2048]{2,1,0:T(8,128)(2,1)S(1)}, bf16[1,768,2048]{2,1,0:T(8,128)(2,1)}, u32[]{:S(2)}) copy-start(bf16[1,768,2048]{2,1,0:T(8,128)(2,1)} %param.13) | copy-start | bytes 9437188
  94.4 1.8 copy-start.13
  94.4 1.9 copy-start.15
  94.4 2.2 copy-start.12
  96.2 1.4 copy-start.11
  96.3 2.0 copy-start.10
  96.8 14.2 %copy-start.4 = (bf16[2,4,4,4,8,640]{5,4,3,2,0,1:T(8,128)(2,1)}, bf16[2,4,4,4,8,640]{5,4,3,2,0,1:T(8,128)(2,1)S(1)}, u32[]{:S(2)}) copy-start(bf16[2,4,4,4,8,640]{5,4,3,2,0,1:T(8,128)(2,1)S(1)} %copy.54) | copy-start | bytes 3932164
  96.8 2.5 copy-start.9
  97.8 13.3 %copy-start.6 = (bf16[2,4,4,4,8,640]{5,4,1,3,0,2:T(8,128)(2,1)}, bf16[2,4,4,4,8,640]{5,4,1,3,0,2:T(8,128)(2,1)S(1)}, u32[]{:S(2)}) copy-start(bf16[2,4,4,4,8,640]{5,4,1,3,0,2:T(8,128)(2,1)S(1)} %copy.53) | copy-start | bytes 3932164
  99.5 11.5 %copy-start.2 = (bf16[2,4,4,4,8,768]{5,4,2,1,0,3:T(8,128)(2,1)}, bf16[2,4,4,4,8,768]{5,4,2,1,0,3:T(8,128)(2,1)S(1)}, u32[]{:S(2)}) copy-start(bf16[2,4,4,4,8,768]{5,4,2,1,0,3:T(8,128)(2,1)S(1)} %copy.55) | copy-start | bytes 4718596
  99.5 4.0 %copy-start.20 = (bf16[1,2048,768]{2,1,0:T(8,128)(2,1)S(1)}, bf16[1,2048,768]{2,1,0:T(8,128)(2,1)}, u32[]{:S(2)}) copy-start(bf16[1,2048,768]{2,1,0:T(8,128)(2,1)} %param.12) | copy-start | bytes 9437188
  100.2 6.7 %copy-start.7 = (bf16[4,2,4,4,8,2048]{5,4,3,2,1,0:T(8,128)(2,1)}, bf16[4,2,4,4,8,2048]{5,4,3,2,1,0:T(8,128)(2,1)S(1)}, u32[]{:S(2)}) copy-start(bf16[4,2,4,4,8,2048]{5,4,3,2,1,0:T(8,128)(2,1)S(1)} %pad_maximum_fusion) | copy-start | bytes 12582916
  103.5 3.4 %copy-start.19 = (bf16[1,2048,768]{2,1,0:T(8,128)(2,1)S(1)}, bf16[1,2048,768]{2,1,0:T(8,128)(2,1)}, u32[]{:S(2)}) copy-start(bf16[1,2048,768]{2,1,0:T(8,128)(2,1)} %param.11) | copy-start | bytes 9437188
  117.6 1.2 copy-start.22
  123.7 6.7 %copy-start.14 = (s32[64,8]{1,0:T(8,128)S(1)}, s32[64,8]{1,0:T(8,128)}, u32[]{:S(2)}) copy-start(s32[64,8]{1,0:T(8,128)} %copy.19.routes) | copy-start | bytes 6148
  123.7 6.9 %copy-start.18 = (s32[64,8]{0,1:T(8,128)S(1)}, s32[64,8]{0,1:T(8,128)}, u32[]{:S(2)}) copy-start(s32[64,8]{0,1:T(8,128)} %param.8) | copy-start | bytes 6148
  123.7 7.1 %copy-start.17 = (f32[64,8]{0,1:T(8,128)S(1)}, f32[64,8]{0,1:T(8,128)}, u32[]{:S(2)}) copy-start(f32[64,8]{0,1:T(8,128)} %param.9) | copy-start | bytes 6148
  123.7 7.5 %copy-start.24 = (bf16[1024,768]{1,0:T(8,128)(2,1)S(1)}, bf16[1024,768]{1,0:T(8,128)(2,1)}, u32[]{:S(2)}) copy-start(bf16[1024,768]{1,0:T(8,128)(2,1)} %get-tuple-element.21) | copy-start | bytes 4718596
  123.7 58.6 %all-to-all-start = ((bf16[128,8,2048]{2,1,0:T(8,128)(2,1)}), bf16[128,8,2048]{2,1,0:T(8,128)(2,1)}, u32[]{:S(2)}, u32[]{:S(2)}) async-start(bf16[128,8,2048]{2,1,0:T(8,128)(2,1)} %convert_bitcast_fusion), calls=%async_computation | async-start | bytes 8388608 | tf_op jit(solution)/shard_map/all_to_all | solution.py:345
  131.3 5.5 %copy-start.21 = (bf16[1,2048,768]{2,1,0:T(8,128)(2,1)S(1)}, bf16[1,2048,768]{2,1,0:T(8,128)(2,1)}, u32[]{:S(2)}) copy-start(bf16[1,2048,768]{2,1,0:T(8,128)(2,1)} %param.12) | copy-start | bytes 9437188
  131.3 5.5 %copy-start.26 = (bf16[1024,768]{1,0:T(8,128)(2,1)S(1)}, bf16[1024,768]{1,0:T(8,128)(2,1)}, u32[]{:S(2)}) copy-start(bf16[1024,768]{1,0:T(8,128)(2,1)} %get-tuple-element.20) | copy-start | bytes 4718596
  141.8 46.1 %copy-start.3 = (bf16[2,4,4,4,8,768]{5,4,2,1,0,3:T(8,128)(2,1)S(1)}, bf16[2,4,4,4,8,768]{5,4,2,1,0,3:T(8,128)(2,1)}, u32[]{:S(2)}) copy-start(bf16[2,4,4,4,8,768]{5,4,2,1,0,3:T(8,128)(2,1)} %copy-done.2) | copy-start | bytes 4718596
  141.8 46.1 %copy-start.5 = (bf16[2,4,4,4,8,640]{5,4,3,2,0,1:T(8,128)(2,1)S(1)}, bf16[2,4,4,4,8,640]{5,4,3,2,0,1:T(8,128)(2,1)}, u32[]{:S(2)}) copy-start(bf16[2,4,4,4,8,640]{5,4,3,2,0,1:T(8,128)(2,1)} %copy-done.4) | copy-start | bytes 3932164
  182.4 57.1 %all-to-all-start.1 = ((bf16[128,8,2048]{2,1,0:T(8,128)(2,1)}), bf16[128,8,2048]{2,1,0:T(8,128)(2,1)}, u32[]{:S(2)}, u32[]{:S(2)}) async-start(bf16[128,8,2048]{2,1,0:T(8,128)(2,1)} %fusion.2), calls=%async_computation.1 | async-start | bytes 8388608 | tf_op jit(solution)/shard_map/all_to_all | solution.py:351
  188.0 2.6 %copy-start.8 = (bf16[4,2,4,4,8,2048]{5,4,3,2,1,0:T(8,128)(2,1)S(1)}, bf16[4,2,4,4,8,2048]{5,4,3,2,1,0:T(8,128)(2,1)}, u32[]{:S(2)}) copy-start(bf16[4,2,4,4,8,2048]{5,4,3,2,1,0:T(8,128)(2,1)} %copy-done.7) | copy-start | bytes 12582916
  188.0 3.1 %copy-start.27 = (bf16[1024,768]{1,0:T(8,128)(2,1)S(1)}, bf16[1024,768]{1,0:T(8,128)(2,1)}, u32[]{:S(2)}) copy-start(bf16[1024,768]{1,0:T(8,128)(2,1)} %get-tuple-element.20) | copy-start | bytes 4718596
  191.0 4.9 %copy-start.25 = (bf16[1024,768]{1,0:T(8,128)(2,1)S(1)}, bf16[1024,768]{1,0:T(8,128)(2,1)}, u32[]{:S(2)}) copy-start(bf16[1024,768]{1,0:T(8,128)(2,1)} %get-tuple-element.21) | copy-start | bytes 4718596
  195.9 4.9 %copy-start.23 = (bf16[1024,768]{1,0:T(8,128)(2,1)S(1)}, bf16[1024,768]{1,0:T(8,128)(2,1)}, u32[]{:S(2)}) copy-start(bf16[1024,768]{1,0:T(8,128)(2,1)} %copy-done.22) | copy-start | bytes 4718596
  213.0 2.7 %copy-start.16 = (bf16[64,2048]{1,0:T(8,128)(2,1)S(1)}, bf16[64,2048]{1,0:T(8,128)(2,1)}, u32[]{:S(2)}) copy-start(bf16[64,2048]{1,0:T(8,128)(2,1)} %cot.1) | copy-start | bytes 786436
  239.5 12.1 %copy-start.1 = (bf16[1,768,2048]{2,1,0:T(8,128)(2,1)S(1)}, bf16[1,768,2048]{2,1,0:T(8,128)(2,1)}, u32[]{:S(2)}) copy-start(bf16[1,768,2048]{2,1,0:T(8,128)(2,1)} %param.13) | copy-start | bytes 9437188

commit v2 on v1

--- a/solution.py
+++ b/solution.py
@@ -265,95 +265,373 @@
     )(tokens, cotangent, routes, weights)
 
 
-def expert_forward(slot_rows, w_gate, w_up, w_down):
-    gate_pre = jnp.dot(slot_rows, w_gate, preferred_element_type=jnp.float32)
-    up_pre = jnp.dot(slot_rows, w_up, preferred_element_type=jnp.float32)
-    hidden = (jax.nn.silu(gate_pre) * up_pre).astype(jnp.bfloat16)
-    output = jnp.dot(hidden, w_down, preferred_element_type=jnp.float32).astype(jnp.bfloat16)
-    return (gate_pre, up_pre, hidden, output)
-
-
-def expert_backward(slot_rows, slot_grads, gate_pre, up_pre, hidden, w_gate, w_up, w_down):
-    contract_last = (((1,), (1,)), ((), ()))
-    contract_first = (((0,), (0,)), ((), ()))
-    hidden_back = lax.dot_general(
-        slot_grads, w_down, contract_last, preferred_element_type=jnp.float32
-    )
-    sigmoid_gate = jax.nn.sigmoid(gate_pre)
-    gate_back = (
-        hidden_back * up_pre * sigmoid_gate * (1.0 + gate_pre * (1.0 - sigmoid_gate))
-    ).astype(jnp.bfloat16)
-    up_back = (hidden_back * gate_pre * sigmoid_gate).astype(jnp.bfloat16)
-    down_grad = lax.dot_general(
-        hidden, slot_grads, contract_first, preferred_element_type=jnp.float32
-    ).astype(jnp.bfloat16)
-    gate_grad = lax.dot_general(
-        slot_rows, gate_back, contract_first, preferred_element_type=jnp.float32
-    ).astype(jnp.bfloat16)
-    up_grad = lax.dot_general(
-        slot_rows, up_back, contract_first, preferred_element_type=jnp.float32
-    ).astype(jnp.bfloat16)
-    input_back = lax.dot_general(
-        gate_back, w_gate, contract_last, preferred_element_type=jnp.float32
-    )
-    input_back = input_back + lax.dot_general(
-        up_back, w_up, contract_last, preferred_element_type=jnp.float32
-    )
-    return (input_back.astype(jnp.bfloat16), gate_grad, up_grad, down_grad)
-
-
-def combine_slots(out_slot, back_slot, route_weights, cotangent):
-    out_float = out_slot.astype(jnp.float32)
-    mixed = jnp.einsum(
-        "tk,tkd->td", route_weights, out_float, precision=lax.Precision.HIGHEST
-    ).astype(jnp.bfloat16)
-    weight_grad = jnp.einsum(
-        "tkd,td->tk", out_float, cotangent.astype(jnp.float32), precision=lax.Precision.HIGHEST
-    )
-    token_grad = jnp.sum(back_slot.astype(jnp.float32), axis=1).astype(jnp.bfloat16)
-    return (mixed, token_grad, weight_grad)
-
-
-def canonical(parts):
-    a, b, c = parts
-    w = [part[4] for part in PARTS]
-    a = a.reshape(2, 4, 4, 4, 8, w[0]).transpose(3, 0, 1, 2, 4, 5)
-    b = b.reshape(2, 4, 4, 4, 8, w[1]).transpose(1, 0, 2, 3, 4, 5)
-    c = c.reshape(2, 4, 4, 4, 8, w[2]).transpose(2, 0, 3, 1, 4, 5)
-    return jnp.concatenate([a, b, c], axis=-1).reshape(1024, 2048)
+def pieces(p):
+    for k in range(8):
+        c, d = k // 4, k % 4
+        if p == 0:
+            yield k * 128, 128, (k,)
+        elif p == 1:
+            yield k * 128, 128, (slice(4 * c, 4 * c + 4), slice(None), d)
+        else:
+            for x in range(4):
+                yield k * 128 + x * 32, 32, (slice(4 * c, 4 * c + 4), d, x)
+
+
+def tiles(cols, body):
+    def step(n, _):
+        body(pl.multiple_of(n * 256, 256), 256)
+        return 0
+
+    lax.fori_loop(0, cols // 256, step, 0)
+    if cols % 256:
+        body(cols - cols % 256, cols % 256)
+
+
+def contract(a, b, da, db):
+    return lax.dot_general(a, b, (((da,), (db,)), ((), ())), preferred_element_type=F32)
+
+
+def expert_kernel(xi, xi1, xi2, ci, ci1, ci2, rwi, sti, wgi, wui, wdi, *refs):
+    mixed, tgrad, vgrad, ggrad, ugrad, dgrad = refs[0:6]
+    back_in = refs[6:13]
+    refs = refs[13:]
+    x, c, rw, st = refs[0:3], refs[3:6], refs[6], refs[7]
+    wg, wu, wd = refs[8:11]
+    ag, au, ah = refs[11:14]
+    hw, gb, ub = refs[14:17], refs[17], refs[18]
+    send = refs[19:26]
+    ring = refs[26:33]
+    line = refs[33:40]
+    wcol, rep, stage = refs[40:43]
+    ld, s4, r4, loc, s5, r5, s6, r6, sg = refs[43:52]
+    co, core = place()
+    loads = [
+        pltpu.make_async_copy(src, dst, ld.at[i])
+        for i, (src, dst) in enumerate(
+            zip((xi, xi1, xi2, rwi, wgi, wui, wdi, ci, ci1, ci2, sti), (*x, rw, wg, wu, wd, *c, st), strict=True)
+        )
+    ]
+    for load in loads:
+        load.start()
+    barrier, count = greet(co, core)
+    own = ((co[0] * 2 + core) * 16 + co[2] * 4 + co[1] + 1).astype(F32)
+    widths = [part[4] for part in PARTS]
+
+    for load in loads[:6]:
+        load.wait()
+
+    def pre(n, _):
+        n0 = pl.multiple_of(n * 256, 256)
+        for w, acc in ((wg, ag), (wu, au)):
+            for p, (_, _, _, c0, cols) in enumerate(PARTS):
+                r = jnp.dot(
+                    x[p][...].reshape(1024, cols), w[c0 : c0 + cols, pl.ds(n0, 256)], preferred_element_type=F32
+                )
+                for row, rows, at in pieces(p):
+                    piece = r[row : row + rows]
+                    at = (*at, *([slice(None)] * (4 - len(at))), pl.ds(n0, 256))
+                    where = acc.at[at]
+                    piece = piece.reshape(where.shape)
+                    where[...] = piece if p == 0 else where[...] + piece
+        return 0
+
+    lax.fori_loop(0, 3, pre, 0)
+
+    lane = lax.broadcasted_iota(jnp.int32, (128, 128), 1)
+    row = lax.broadcasted_iota(jnp.int32, (128, 128), 0)
+    spread = jnp.where((row < 8) & (lane < 32) & (lane % 8 == row), 1.0, 0.0).astype(BF16)
+
+    def weigh(k, _):
+        route = jnp.dot(rw[k], spread, preferred_element_type=F32)
+        taken = jnp.where((route == own) & (lane >= 8), rw[k].astype(F32), 0.0)
+        wcol[k] = jnp.broadcast_to(jnp.sum(taken, axis=1, keepdims=True), (128, 128))
+        rep[k] = route
+        return 0
+
+    lax.fori_loop(0, 8, weigh, 0)
+
+    def activate(i, _):
+        k, y = i // 4, i % 4
+        rows = pl.ds(pl.multiple_of(y * 32, 32), 32)
+        g, u = ag[k, y].reshape(32, 768), au[k, y].reshape(32, 768)
+        w = wcol[k, rows, 0:1]
+        ah[k, y] = (g * jax.nn.sigmoid(g) * u * w).reshape(4, 8, 768)
+        return 0
+
+    lax.fori_loop(0, 32, activate, 0)
+
+    def ordered(acc, out, p):
+        for row, rows, at in pieces(p):
+            out[row : row + rows, :] = acc[at].reshape(rows, 768).astype(BF16)
+
+    for p in range(3):
+        ordered(ah, hw[p], p)
+    pl.semaphore_wait(barrier, count)
+    loads[6].wait()
+
+    sent = []
+
+    def slot_ends(p):
+        axis = PARTS[p][2]
+        for dc in (0, 1):
+            for d in (1, 3, 2, 0):
+                if dc == 0 and d == 0:
+                    continue
+                there, other = (co[axis] + d) % 4, (core + dc) % 2
+                yield dc * 4 + d, other * 4 + there, device(moved(co, axis, there), other)
+
+    slot_sent = {}
+
+    def slot_start(p, n):
+        me = core * 4 + co[PARTS[p][2]]
+        src, dst = send[n], back_in[n]
+        copies = [remote(src.at[k], dst.at[me], s4.at[n, i], r4.at[n, me], to) for i, k, to in slot_ends(p)]
+        for copy in copies:
+            copy.start()
+        local = pltpu.make_async_copy(src.at[me], dst.at[me], loc.at[n])
+        local.start()
+        slot_sent[n] = (copies, local)
+
+    def slot_finish(p, n):
+        copies, local = slot_sent[n]
+        local.wait()
+        for copy in copies:
+            copy.wait_send()
+        for i, k, to in slot_ends(p):
+            remote(send[n].at[k], back_in[n].at[k], s4.at[n, i], r4.at[n, k], to).wait_recv()
+
+    for p, (_, _, _, c0, cols) in enumerate(PARTS):
+
+        def forward(n0, width, p=p, c0=c0):
+            r = jnp.dot(hw[p][...], wd[:, pl.ds(c0 + n0, width)], preferred_element_type=F32)
+            send[p][:, :, pl.ds(n0, width)] = r.astype(BF16).reshape(8, 128, width)
+
+        tiles(cols, forward)
+        slot_start(p, p)
+
+    for load in loads[7:]:
+        load.wait()
+
+    def hidden_back(n, _):
+        n0 = pl.multiple_of(n * 256, 256)
+        for p, (_, _, _, c0, cols) in enumerate(PARTS):
+            r = contract(c[p][...].reshape(1024, cols), wd[pl.ds(n0, 256), c0 : c0 + cols], 1, 1)
+            for row, rows, at in pieces(p):
+                piece = r[row : row + rows]
+                at = (*at, *([slice(None)] * (4 - len(at))), pl.ds(n0, 256))
+                where = ah.at[at]
+                piece = piece.reshape(where.shape)
+                where[...] = piece if p == 0 else where[...] + piece
+        return 0
+
+    lax.fori_loop(0, 3, hidden_back, 0)
+    lane32 = lax.broadcasted_iota(jnp.int32, (32, 128), 1)
+
+    def derive(i, _):
+        k, y = i // 4, i % 4
+        rows = pl.ds(pl.multiple_of(y * 32, 32), 32)
+        g, u, h = ag[k, y].reshape(32, 768), au[k, y].reshape(32, 768), ah[k, y].reshape(32, 768)
+        w = wcol[k, rows, 0:1]
+        s = jax.nn.sigmoid(g)
+        silu = g * s
+        value = jnp.sum(silu * u * h, axis=1, keepdims=True)
+        high = value.astype(BF16).astype(F32)
+        match = rep[k, rows] == own
+        both = jnp.where(lane32 < 8, high, jnp.where(lane32 < 16, value - high, 0.0))
+        send[6][k, rows] = jnp.where(match, both, 0.0).astype(BF16)
+        h = h * w
+        ag[k, y] = (h * u * s * (1.0 + g * (1.0 - s))).reshape(4, 8, 768)
+        au[k, y] = (h * silu).reshape(4, 8, 768)
+        return 0
+
+    lax.fori_loop(0, 32, derive, 0)
+    slot_start(0, 6)
+    for p, (_, _, _, c0, cols) in enumerate(PARTS):
+        ordered(ag, gb, p)
+        ordered(au, ub, p)
+
+        def backward(n0, width, p=p, c0=c0):
+            rows = pl.ds(c0 + n0, width)
+            r = contract(gb[...], wg[rows, :], 1, 1) + contract(ub[...], wu[rows, :], 1, 1)
+            send[3 + p][:, :, pl.ds(n0, width)] = r.astype(BF16).reshape(8, 128, width)
+
+        tiles(cols, backward)
+        slot_start(p, 3 + p)
+
+    def neighbour(p, d):
+        a2 = PARTS[p][1]
+        return device(moved(co, a2, (co[a2] + d) % 4), core)
+
+    def ring_copy(p, n, chunk, kind):
+        to_right = kind in (0, 2, 3)
+        return remote(send[n].at[chunk], ring[n].at[kind], s5.at[n, kind], r5.at[n, kind], neighbour(p, 1 if to_right else 3))
+
+    def go(copy):
+        copy.start()
+        sent.append(copy)
+
+    def ring_first(p, n):
+        slot_finish(p, n)
+        cols = send[n].shape[-1]
+        me = co[PARTS[p][1]]
+        for d in (2, 1, 3, 0):
+            g = (me + d) % 4
+            copy = pltpu.make_async_copy(
+                back_in[n].at[:, pl.ds(pl.multiple_of(g * 32, 32), 32)], stage.at[:, :, pl.ds(0, cols)], loc.at[n]
+            )
+            copy.start()
+            copy.wait()
+            r = jnp.dot(st[p, g], stage[:, :, 0:cols].reshape(256, cols), preferred_element_type=F32)
+            send[n][pl.ds(2 * g, 2)] = r.astype(BF16).reshape(2, 128, cols)
+            if d == 2:
+                go(ring_copy(p, n, 2 * g, 0))
+                go(ring_copy(p, n, 2 * g + 1, 1))
+            if d == 1:
+                go(ring_copy(p, n, 2 * g + 1, 3))
+            if d == 3:
+                go(ring_copy(p, n, 2 * g, 4))
+
+    def ring_pass(p, n):
+        me = co[PARTS[p][1]]
+        for kind, chunk, out in ((0, 2 * ((me + 1) % 4), 2), (1, 2 * ((me + 3) % 4) + 1, 5)):
+            ring_copy(p, n, chunk, kind).wait_recv()
+            send[n][chunk] = (send[n][chunk].astype(F32) + ring[n][kind].astype(F32)).astype(BF16)
+            go(ring_copy(p, n, chunk, out))
+
+    def line_copy(p, n, i, d):
+        a1, a2 = PARTS[p][:2]
+        rows = pl.ds(pl.multiple_of((i % 2) * 64, 64), 64)
+        return rows, remote(
+            send[n].at[2 * co[a2] + i // 2, rows],
+            line[n].at[co[a1]],
+            s6.at[n, d - 1],
+            r6.at[n, co[a1]],
+            device(moved(co, a1, (co[a1] + d) % 4), core),
+        )
+
+    def line_first(p, n):
+        a1, a2 = PARTS[p][:2]
+        for h in (0, 1):
+            chunk = 2 * co[a2] + h
+            ring_copy(p, n, chunk, 2 + h).wait_recv()
+            ring_copy(p, n, chunk, 4 + h).wait_recv()
+            total = send[n][chunk].astype(F32) + ring[n][2 + h].astype(F32) + ring[n][4 + h].astype(F32)
+            send[n][chunk] = total.astype(BF16)
+        for d in (2, 1, 3):
+            go(line_copy(p, n, (co[a1] + d) % 4, d)[1])
+
+    def line_last(p, n):
+        a1, a2 = PARTS[p][:2]
+        i = co[a1]
+        rows = pl.ds(pl.multiple_of((i % 2) * 64, 64), 64)
+        total = send[n][2 * co[a2] + i // 2, rows].astype(F32)
+        for d in (1, 2, 3):
+            j = (i + d) % 4
+            got = line[n].at[j]
+            remote(got, got, s6.at[n, d - 1], r6.at[n, j], device(moved(co, a1, j), core)).wait_recv()
+            total = total + line[n][j].astype(F32)
+        return total
+
+    outs = [(p, p) for p in range(3)]
+    backs = [(0, 6)] + [(p, 3 + p) for p in range(3)]
+    for item in outs:
+        ring_first(*item)
+    for p, (_, _, _, c0, cols) in enumerate(PARTS):
+
+        def down(n, _, p=p, c0=c0, cols=cols):
+            n0 = pl.ds(pl.multiple_of(n * 256, 256), 256)
+            wd[n0, c0 : c0 + cols] = contract(hw[p][:, n0], c[p][...].reshape(1024, cols), 0, 0).astype(BF16)
+            return 0
+
+        lax.fori_loop(0, 3, down, 0)
+    grads = [pltpu.make_async_copy(wd, dgrad, sg.at[0])]
+    grads[0].start()
+    for item in outs:
+        ring_pass(*item)
+    for item in backs:
+        ring_first(*item)
+    for item in outs:
+        line_first(*item)
+
+    def rows_of(p):
+        c0, cols = PARTS[p][3:]
+
+        def gate(n0, width):
+            part = x[p][:, :, pl.ds(n0, width)].reshape(1024, width)
+            rows = pl.ds(c0 + n0, width)
+            wg[rows, :] = contract(part, gb[...], 0, 0).astype(BF16)
+            wu[rows, :] = contract(part, ub[...], 0, 0).astype(BF16)
+
+        tiles(cols, gate)
+        for i, (src, dst) in enumerate(((wg, ggrad), (wu, ugrad))):
+            copy = pltpu.make_async_copy(src.at[pl.ds(c0, cols)], dst.at[pl.ds(c0, cols)], sg.at[1 + 2 * p + i])
+            copy.start()
+            grads.append(copy)
+
+    rows_of(2)
+    for item in backs:
+        ring_pass(*item)
+    ordered(ag, gb, 1)
+    ordered(au, ub, 1)
+    rows_of(1)
+    for item in backs:
+        line_first(*item)
+    ordered(ag, gb, 0)
+    ordered(au, ub, 0)
+    rows_of(0)
+    for p, (_, _, _, c0, cols) in enumerate(PARTS):
+        mixed[:, c0 : c0 + cols] = line_last(p, p).astype(BF16)
+        tgrad[:, c0 : c0 + cols] = line_last(p, 3 + p).astype(BF16)
+    vgrad[...] = line_last(0, 6)
+    for copy in sent:
+        copy.wait_send()
+    for copy in grads:
+        copy.wait()
+
+
+def expert(out, gate_weight, up_weight, down_weight):
+    widths = [part[4] for part in PARTS]
+    shape = jax.ShapeDtypeStruct
+    any_, vmem = pl.BlockSpec(memory_space=pl.ANY), pl.BlockSpec(memory_space=pltpu.VMEM)
+    items = widths * 2 + [128]
+    outs = [
+        shape((64, 2048), BF16),
+        shape((64, 2048), BF16),
+        shape((64, 128), F32),
+        shape((2048, 768), BF16),
+        shape((2048, 768), BF16),
+        shape((768, 2048), BF16),
+    ] + [shape((8, 128, w), BF16) for w in items]
+    slots = [pltpu.VMEM((8, 128, w), BF16) for w in widths]
+    dma = pltpu.SemaphoreType.DMA
+    got = pl.pallas_call(
+        expert_kernel,
+        out_shape=outs,
+        in_specs=[any_] * 11,
+        out_specs=[vmem] * 3 + [any_] * 10,
+        scratch_shapes=slots * 2
+        + [pltpu.VMEM((8, 128, 128), BF16), pltpu.VMEM((3, 4, 256, 256), BF16)]
+        + [pltpu.VMEM((2048, 768), BF16)] * 2
+        + [pltpu.VMEM((768, 2048), BF16)]
+        + [pltpu.VMEM((8, 4, 4, 8, 768), F32)] * 3
+        + [pltpu.VMEM((1024, 768), BF16)] * 5
+        + [pltpu.VMEM((8, 128, w), BF16) for w in items]
+        + [pltpu.VMEM((6, 128, w), BF16) for w in items]
+        + [pltpu.VMEM((4, 64, w), BF16) for w in items]
+        + [pltpu.VMEM((8, 128, 128), F32)] * 2
+        + [pltpu.VMEM((8, 32, 768), BF16)]
+        + [dma((11,)), dma((7, 8)), dma((7, 8)), dma((7,)), dma((7, 6)), dma((7, 6)), dma((7, 3)), dma((7, 4)), dma((7,))],
+        compiler_params=pltpu.CompilerParams(
+            collective_id=1, has_side_effects=True, vmem_limit_bytes=62 * 2**20
+        ),
+    )(*out, gate_weight, up_weight, down_weight)
+    return got[:6]
 
 
 def per_device(tokens, routes, route_weights, cotangent, gate_weight, up_weight, down_weight):
     out = dispatch(tokens, cotangent, routes, route_weights)
-    slot_rows, slot_cots = canonical(out[0:3]), canonical(out[3:6])
-    extra = out[6].reshape(2, 4, 4, 4, 8, 128).transpose(3, 0, 1, 2, 4, 5).reshape(1024, 128).astype(jnp.float32)
-    own = lax.axis_index(("node", "rail")) + 1
-    weight = jnp.sum(
-        jnp.where(extra[:, :8] == own.astype(jnp.float32), extra[:, 8:16] + extra[:, 16:24] + extra[:, 24:32], 0.0), axis=1
-    )
-    slot_grads = (weight[:, None] * slot_cots.astype(jnp.float32)).astype(jnp.bfloat16)
-    token_count, model_width = tokens.shape
-    top_count = routes.shape[1]
-    experts, capacity = 128, 8
-    flat_routes = routes.reshape(-1)
-    onehot = (flat_routes[:, None] == jnp.arange(experts, dtype=jnp.int32)[None, :]).astype(jnp.int32)
-    position = jnp.sum((jnp.cumsum(onehot, axis=0) - onehot) * onehot, axis=1)
-    slot_index = flat_routes * capacity + position
-    w_gate, w_up, w_down = gate_weight[0], up_weight[0], down_weight[0]
-    gate_pre, up_pre, hidden, output = expert_forward(slot_rows, w_gate, w_up, w_down)
-    names = ("node", "rail")
-    out_home = lax.all_to_all(
-        output.reshape(experts, capacity, model_width), names, split_axis=0, concat_axis=0, tiled=True
-    )
-    input_back, gate_grad, up_grad, down_grad = expert_backward(
-        slot_rows, slot_grads, gate_pre, up_pre, hidden, w_gate, w_up, w_down
-    )
-    back_home = lax.all_to_all(
-        input_back.reshape(experts, capacity, model_width), names, split_axis=0, concat_axis=0, tiled=True
-    )
-    out_slot = out_home.reshape(-1, model_width)[slot_index].reshape(token_count, top_count, model_width)
-    back_slot = back_home.reshape(-1, model_width)[slot_index].reshape(token_count, top_count, model_width)
-    mixed, token_grad, weight_grad = combine_slots(out_slot, back_slot, route_weights, cotangent)
+    mixed, token_grad, value, gate_grad, up_grad, down_grad = expert(out, gate_weight[0], up_weight[0], down_weight[0])
+    weight_grad = value[:, 0:8] + value[:, 8:16]
     return (mixed, token_grad, weight_grad, gate_grad[None], up_grad[None], down_grad[None])
 
 

time: 252 us -> 216 us (0.86); the launches traced: 252 us -> 212 us
  Pallas kernels: 90.8 us -> 195 us
  waiting for transfers between devices: 62.3 us -> 0 us
  matrix products: 46.9 us -> 0 us
  local copies, waits for them, and re-layouts: 31.3 us -> 15.4 us
  starting transfers between devices: 11.9 us -> 0 us
  other arithmetic: 7.29 us -> 0.91 us
    pallas_call x0 -> x1, Pallas kernels: none -> 104 us  [expert(): pl.pallas_call(expert_kernel, out_shape=outs, in_specs=[any_] * 11, out_s...]
    all_to_all x2 -> x0, waiting for transfers between devices: 62.3 us -> none  [the longest x1 40.6 us: per_device(): lax.all_to_all(output.reshape(experts, capacity, model_width), names, spl...]
    dot_general x11 -> x0, matrix products: 46.9 us -> none  [the longest x1 6.5 us: expert_backward(): lax.dot_general(slot_grads, w_down, contract_last, preferred_element_type...]
    gather x2 -> x0, local copies, waits for them, and re-layouts: 15.5 us -> none  [the longest x1 8.34 us: per_device(): back_home.reshape(-1, model_width)[slot_index]]
    all_to_all x2 -> x0, starting transfers between devices: 11.9 us -> none  [the longest x1 6.7 us: per_device(): lax.all_to_all(output.reshape(experts, capacity, model_width), names, spl...]
    reduce_sum x3 -> x0, other arithmetic: 4.58 us -> none  [the longest x1 3.72 us: combine_slots(): jnp.sum(back_slot.astype(jnp.float32), axis=1).astype(jnp.bfloat16)]
    unnamed x60 -> x12, local copies, waits for them, and re-layouts: 11.3 us -> 15.4 us
  transfers between devices with their start and end apart: 2 -> 0, of which waited for: 2 -> 0; matrix products, arithmetic and copies ran while one was open for 16% -> 0% of each run, Pallas kernels for 0% -> 0%
where the time goes in v2:
time: 216 us; the launch traced here: 212 us
  Pallas kernels  195 us (90%)
  local copies, waits for them, and re-layouts  15.4 us (7%)
    pallas_call x1, Pallas kernels, expert(): pl.pallas_call(expert_kernel, out_shape=outs, in_specs=[any_] * 11, out_s...  104 us
    pallas_call x1, Pallas kernels, dispatch(): pl.pallas_call(dispatch_kernel, out_shape=outs, in_specs=[vmem] * 4, out_...  90.9 us
    unnamed x12, local copies, waits for them, and re-layouts  15.4 us

profile of v2, /device:TPU:7, one launch (start us, length us, event | category | flops | bytes accessed | tf_op | source)
XLA Modules:
  0.0 212.0 jit_solution(1525832111644770141)
XLA Ops:
  0.6 1.4 copy.13.routes
  2.0 1.4 copy.14.weights
  3.4 90.9 %shard_map.118 = (bf16[8,128,768]{2,1,0:T(8,128)(2,1)}, bf16[8,128,640]{2,1,0:T(8,128)(2,1)}, bf16[8,128,640]{2,1,0:T(8,128)(2,1)}, bf16[8,128,768]{2,1,0:T(8,12...) custom-call(bf16[64,2048]{1,0:T(8,128)(2,1)} %tok.1, ...), custom_call_target="tpu_custom_call" | custom-call | tf_op jit(solution)/shard_map/pallas_call | solution.py:255
  94.3 104.2 %shard_map.119 = (bf16[64,2048]{1,0:T(8,128)(2,1)}, bf16[64,2048]{1,0:T(8,128)(2,1)}, f32[64,128]{1,0:T(8,128)}, bf16[2048,768]{1,0:T(8,128)(2,1)}, bf16[2048,76...) custom-call(bf16[8,128,768]{2,1,0:T(8,128)(2,1)} %get-tuple-element., ...), custom_call_target="tpu_custom_call" | custom-call | tf_op jit(solution)/shard_map/pallas_call | solution.py:607
  198.5 0.9 slice_add_fusion
  199.4 0.7 copy.15
  200.1 1.7 copy.21
  201.7 1.7 copy.22
  203.4 0.0 copy-start.1
  203.4 3.9 %copy.23 = bf16[1,2048,768]{2,1,0:T(8,128)(2,1)} copy(bf16[1,2048,768]{2,1,0:T(8,128)(2,1)} %bitcast.11) | data formatting | bytes 6291456
  207.3 0.0 copy-done.1
  207.3 0.0 copy-start
  207.3 1.7 copy.24
  209.0 1.4 copy-done
  210.3 1.7 copy.25
Async XLA Ops:
  203.4 3.9 %copy-start.1 = (bf16[2048,768]{1,0:T(8,128)(2,1)S(1)}, bf16[2048,768]{1,0:T(8,128)(2,1)}, u32[]{:S(2)}) copy-start(bf16[2048,768]{1,0:T(8,128)(2,1)} %get-tuple-element.32) | copy-start | bytes 9437188
  207.3 3.0 %copy-start = (bf16[768,2048]{1,0:T(8,128)(2,1)S(1)}, bf16[768,2048]{1,0:T(8,128)(2,1)}, u32[]{:S(2)}) copy-start(bf16[768,2048]{1,0:T(8,128)(2,1)} %get-tuple-element.33) | copy-start | bytes 9437188

commit v3 on v0

v3 whole, which is shorter than its diff:
```python
import jax
import jax.numpy as jnp
from jax import lax
from jax.experimental import pallas as pl
from jax.experimental.pallas import tpu as pltpu
from jax.sharding import PartitionSpec as P

MESH = pl.DeviceIdType.MESH
F32, BF16 = jnp.float32, jnp.bfloat16
PARTS = ((0, 1, 2, 0, 768), (1, 2, 0, 768, 640), (2, 0, 1, 1408, 640))


def place():
    node, rail = lax.axis_index("node"), lax.axis_index("rail")
    return (node // 2, rail % 4, rail // 4), node % 2


def moved(co, axis, value):
    return tuple(value if i == axis else v for i, v in enumerate(co))


def device(co, core):
    return (co[0] * 2 + core, co[2] * 4 + co[1])


def remote(src, dst, send, recv, target):
    return pltpu.make_async_remote_copy(
        src_ref=src, dst_ref=dst, send_sem=send, recv_sem=recv, device_id=target, device_id_type=MESH
    )


def greet(co, core):
    barrier = pltpu.get_barrier_semaphore()
    targets = [device(co, 1 - core)]
    for axis in range(3):
        for step in (1, 2, 3):
            there = moved(co, axis, (co[axis] + step) % 4)
            targets += [device(there, core), device(there, 1 - core)]
    for target in targets:
        pl.semaphore_signal(barrier, inc=1, device_id=target, device_id_type=MESH)
    return barrier, len(targets)


def one_hot(table, co, slot_axis):
    expert = lax.broadcasted_iota(jnp.int32, (128, 256), 0)
    lane = lax.broadcasted_iota(jnp.int32, (128, 256), 1)
    core, along = lane // 128, (lane // 32) % 4
    there = moved(co, slot_axis, along)
    owner = (there[0] * 2 + core) * 16 + there[2] * 4 + there[1]
    spread = jnp.dot(table, jnp.where(expert == owner, 1.0, 0.0).astype(BF16), preferred_element_type=F32)
    row = lax.broadcasted_iota(jnp.int32, (256, 256), 0)
    lane = lax.broadcasted_iota(jnp.int32, (256, 256), 1)
    wanted = jnp.where(row // 64 == (lane // 8) % 4, lane % 8 + 1, -1).astype(F32)
    return jnp.where(spread == wanted, 1.0, 0.0).astype(BF16)


def pieces(p):
    for k in range(8):
        c, d = k // 4, k % 4
        if p == 0:
            yield k * 128, 128, (k,)
        elif p == 1:
            yield k * 128, 128, (slice(4 * c, 4 * c + 4), slice(None), d)
        else:
            for x in range(4):
                yield k * 128 + x * 32, 32, (slice(4 * c, 4 * c + 4), d, x)


def tiles(cols, body):
    def step(n, _):
        body(pl.multiple_of(n * 256, 256), 256)
        return 0

    lax.fori_loop(0, cols // 256, step, 0)
    if cols % 256:
        body(cols - cols % 256, cols % 256)


def contract(a, b, da, db):
    return lax.dot_general(a, b, (((da,), (db,)), ((), ())), preferred_element_type=F32)


def route_tables(routes, weights):
    lanes = lax.broadcasted_iota(jnp.int32, (64, 128), 1).astype(F32)
    ids = routes.astype(F32).astype(BF16)
    rows8 = lax.broadcasted_iota(jnp.int32, (8, 128), 0)
    named = jnp.zeros((64, 128), F32)
    for k in range(8):
        pick = jnp.where(rows8 == k, 1.0, 0.0).astype(BF16)
        named = named + jnp.where(contract(ids, pick, 0, 0) == lanes, 1.0, 0.0)
    row = lax.broadcasted_iota(jnp.int32, (64, 64), 0)
    col = lax.broadcasted_iota(jnp.int32, (64, 64), 1)
    upto = jnp.where(col <= row, 1.0, 0.0).astype(BF16)
    counted = jnp.dot(upto, named.astype(BF16), preferred_element_type=F32)
    table = (counted * named).astype(BF16)
    high = weights.astype(BF16)
    mid = (weights - high.astype(F32)).astype(BF16)
    low = (weights - high.astype(F32) - mid.astype(F32)).astype(BF16)
    lane8 = lax.broadcasted_iota(jnp.int32, (8, 128), 1)
    extra = jnp.zeros((64, 128), F32)
    for i, part in enumerate(((routes + 1).astype(F32).astype(BF16), high, mid, low)):
        extra = extra + contract(part, jnp.where(lane8 == rows8 + 8 * i, 1.0, 0.0).astype(BF16), 0, 0)
    return table, extra.astype(BF16)


def moe_kernel(tok, cot, routes, weights, wgi, wui, wdi, *refs):
    ggrad, ugrad, dgrad = refs[0:3]
    ring, line = refs[3:10], refs[10:17]
    refs = refs[17:]
    xb, cb, vr, qb, rwb = refs[0:3], refs[3:6], refs[6], refs[7:10], refs[10]
    send = refs[11:18]
    x, c, rw, st = refs[18:21], refs[21:24], refs[24], refs[25]
    wg, wu, wd = refs[26:29]
    ag, au, ah = refs[29:32]
    hw, gb, ub, wcol = refs[32:35], refs[35], refs[36], refs[37]
    s1, r1, s2, r2, s3, r3, loc3, ld, s4, r4, loc4, s5, r5, s6, r6, sg, ls = refs[38:55]
    co, core = place()
    own = ((co[0] * 2 + core) * 16 + co[2] * 4 + co[1] + 1).astype(F32)
    barrier, count = greet(co, core)
    loads = [pltpu.make_async_copy(src, dst, ld.at[i]) for i, (src, dst) in enumerate(((wgi, wg), (wui, wu), (wdi, wd)))]

    def half_rows(i):
        return pl.ds(pl.multiple_of((i % 2) * 64, 64), 64)

    def source(p, i2, i1):
        return 2 * i2 + i1 // 2, half_rows(i1)

    rows = [(xb[p], p, p) for p in range(3)]
    grads = [(cb[p], p, 3 + p) for p in range(3)]
    tables = [(qb[p], p, 6 + p) for p in range(3)] + [(rwb, 0, 9)]

    def put(buf, p, value):
        a1, a2 = PARTS[p][:2]
        chunk, at = source(p, co[a2], co[a1])
        buf[chunk, at] = value

    flying = {}

    def launch(n, copies):
        for copy in copies:
            copy.start()
        flying.setdefault(n, []).extend(copies)

    def landed(n):
        for copy in flying.pop(n):
            copy.wait_send()

    def first_start(buf, p, n):
        a1, a2 = PARTS[p][:2]
        chunk, at = source(p, co[a2], co[a1])
        mine = buf.at[chunk, at]
        launch(n, [
            remote(mine, mine, s1.at[n, d - 1], r1.at[n, co[a1]], device(moved(co, a1, (co[a1] + d) % 4), core))
            for d in (2, 1, 3)
        ])

    def first_wait(buf, p, n):
        a1, a2 = PARTS[p][:2]
        for d in (1, 2, 3):
            i = (co[a1] + d) % 4
            chunk, at = source(p, co[a2], i)
            got = buf.at[chunk, at]
            remote(got, got, s1.at[n, d - 1], r1.at[n, i], device(moved(co, a1, i), core)).wait_recv()

    def second_copy(buf, p, n, block, h, right, number):
        a2 = PARTS[p][1]
        part = buf.at[2 * block + h]
        target = device(moved(co, a2, (co[a2] + (1 if right else 3)) % 4), core)
        return remote(part, part, s2.at[n, number], r2.at[n, block, h], target)

    def second_start(buf, p, n):
        me = co[PARTS[p][1]]
        launch(n, [
            second_copy(buf, p, n, me, 0, True, 0),
            second_copy(buf, p, n, me, 1, False, 1),
            second_copy(buf, p, n, me, 1, True, 2),
            second_copy(buf, p, n, me, 0, False, 3),
        ])

    def second_wait(buf, p, n, d, h):
        second_copy(buf, p, n, (co[PARTS[p][1]] + d) % 4, h, True, 0).wait_recv()

    def relay(buf, p, n):
        me = co[PARTS[p][1]]
        second_wait(buf, p, n, 3, 0)
        launch(n, [second_copy(buf, p, n, (me + 3) % 4, 0, True, 4)])
        second_wait(buf, p, n, 1, 1)
        launch(n, [second_copy(buf, p, n, (me + 1) % 4, 1, False, 5)])

    def rest_wait(buf, p, n):
        for d, h in ((3, 1), (1, 0), (2, 0), (2, 1)):
            second_wait(buf, p, n, d, h)

    for p, (_, _, _, c0, cols) in enumerate(PARTS):
        put(xb[p], p, tok[:, c0 : c0 + cols])
    pl.semaphore_wait(barrier, count)
    for item in rows:
        first_start(*item)
    table, extra = route_tables(routes[...], weights[...])
    for p in range(3):
        put(qb[p], p, table)
    put(rwb, 0, extra)
    for item in tables:
        first_start(*item)
    for p, (_, _, _, c0, cols) in enumerate(PARTS):
        put(cb[p], p, cot[:, c0 : c0 + cols])
    for item in grads:
        first_start(*item)
    for load in loads:
        load.start()
    for item in rows + tables + grads:
        first_wait(*item)
        second_start(*item)
    for item in tables + rows:
        relay(*item)
    for item in tables:
        rest_wait(*item)
    for p, (_, _, slot_axis, _, _) in enumerate(PARTS):

        def build(g, _, p=p, slot_axis=slot_axis):
            st[p, g] = one_hot(qb[p][pl.ds(2 * g, 2)].reshape(256, 128), co, slot_axis)
            return 0

        lax.fori_loop(0, 4, build, 0)

    def pick(buf, out, p):
        cols = buf.shape[-1]

        def step(g, _):
            r = contract(st[p, g], buf[pl.ds(2 * g, 2)].reshape(256, cols), 0, 0)
            out[:, pl.ds(pl.multiple_of(g * 32, 32), 32), :] = r.astype(BF16).reshape(8, 32, cols)
            return 0

        lax.fori_loop(0, 4, step, 0)

    def slot_ends(p):
        axis = PARTS[p][2]
        for dc in (0, 1):
            for d in (2, 1, 3, 0):
                if dc == 0 and d == 0:
                    continue
                there, other = (co[axis] + d) % 4, (core + dc) % 2
                yield dc * 4 + d, other * 4 + there, device(moved(co, axis, there), other)

    moving = {}

    def slot_start(way, src, dst, p, n):
        me = core * 4 + co[PARTS[p][2]]
        ss, rs, loc = (s3, r3, loc3) if way == 0 else (s4, r4, loc4)
        copies = [remote(src.at[k], dst.at[me], ss.at[n, i], rs.at[n, me], to) for i, k, to in slot_ends(p)]
        for copy in copies:
            copy.start()
        local = pltpu.make_async_copy(src.at[me], dst.at[me], loc.at[n])
        local.start()
        moving[way, n] = (src, dst, p, copies, local, ss, rs)

    def slot_sent(way, n):
        for copy in moving[way, n][3]:
            copy.wait_send()
        moving[way, n][4].wait()

    def slot_got(way, n):
        src, dst, p, _, _, ss, rs = moving[way, n]
        for i, k, to in slot_ends(p):
            remote(src.at[k], dst.at[k], ss.at[n, i], rs.at[n, k], to).wait_recv()

    pick(rwb, send[6], 0)
    slot_start(0, send[6], rw, 0, 6)
    for p in range(3):
        rest_wait(*rows[p])
        pick(xb[p], send[p], p)
        landed(p)
        slot_start(0, send[p], x[p], p, p)
    for item in grads:
        relay(*item)
    for p in range(3):
        rest_wait(*grads[p])
        pick(cb[p], send[3 + p], p)
        landed(3 + p)
        slot_start(0, send[3 + p], c[p], p, 3 + p)
    for n in range(6, 10):
        landed(n)

    for n in (6, 0, 1, 2):
        slot_sent(0, n)
        slot_got(0, n)
    for load in loads:
        load.wait()

    def gather_into(acc, r, p, n0):
        for row, count, at in pieces(p):
            at = (*at, *([slice(None)] * (4 - len(at))), pl.ds(n0, 256))
            where = acc.at[at]
            piece = r[row : row + count].reshape(where.shape)
            where[...] = piece if p == 0 else where[...] + piece

    def pre(n, _):
        n0 = pl.multiple_of(n * 256, 256)
        for w, acc in ((wg, ag), (wu, au)):
            for p, (_, _, _, c0, cols) in enumerate(PARTS):
                part = x[p][...].reshape(1024, cols)
                gather_into(acc, jnp.dot(part, w[c0 : c0 + cols, pl.ds(n0, 256)], preferred_element_type=F32), p, n0)
        return 0

    lax.fori_loop(0, 3, pre, 0)

    lane = lax.broadcasted_iota(jnp.int32, (128, 128), 1)
    row = lax.broadcasted_iota(jnp.int32, (128, 128), 0)
    spread = jnp.where((row < 8) & (lane < 32) & (lane % 8 == row), 1.0, 0.0).astype(BF16)

    def weigh(k, _):
        route = jnp.dot(rw[k], spread, preferred_element_type=F32)
        taken = jnp.where((route == own) & (lane >= 8), rw[k].astype(F32), 0.0)
        wcol[k] = jnp.broadcast_to(jnp.sum(taken, axis=1, keepdims=True), (128, 128))
        return 0

    lax.fori_loop(0, 8, weigh, 0)

    def rows32(y):
        return pl.ds(pl.multiple_of(y * 32, 32), 32)

    def activate(i, _):
        k, y = i // 4, i % 4
        g, u = ag[k, y].reshape(32, 768), au[k, y].reshape(32, 768)
        w = wcol[k, rows32(y), 0:1]
        ah[k, y] = (g * jax.nn.sigmoid(g) * u * w).reshape(4, 8, 768)
        return 0

    lax.fori_loop(0, 32, activate, 0)

    def ordered(acc, out, p):
        for row, count, at in pieces(p):
            out[row : row + count, :] = acc[at].reshape(count, 768).astype(BF16)

    for p, (_, _, _, c0, cols) in enumerate(PARTS):
        ordered(ah, hw[p], p)

        def forward(n0, width, p=p, c0=c0):
            r = jnp.dot(hw[p][...], wd[:, pl.ds(c0 + n0, width)], preferred_element_type=F32)
            send[p][:, :, pl.ds(n0, width)] = r.astype(BF16).reshape(8, 128, width)

        tiles(cols, forward)
        slot_start(1, send[p], xb[p], p, p)

    for n in (3, 4, 5):
        slot_sent(0, n)
        slot_got(0, n)

    def hidden_back(n, _):
        n0 = pl.multiple_of(n * 256, 256)
        for p, (_, _, _, c0, cols) in enumerate(PARTS):
            r = contract(c[p][...].reshape(1024, cols), wd[pl.ds(n0, 256), c0 : c0 + cols], 1, 1)
            gather_into(ah, r, p, n0)
        return 0

    lax.fori_loop(0, 3, hidden_back, 0)
    lane32 = lax.broadcasted_iota(jnp.int32, (32, 128), 1)

    def derive(i, _):
        k, y = i // 4, i % 4
        g, u, h = ag[k, y].reshape(32, 768), au[k, y].reshape(32, 768), ah[k, y].reshape(32, 768)
        w = wcol[k, rows32(y), 0:1]
        s = jax.nn.sigmoid(g)
        silu = g * s
        value = jnp.sum(silu * u * h, axis=1, keepdims=True)
        high = value.astype(BF16).astype(F32)
        match = jnp.dot(rw[k, rows32(y)], spread, preferred_element_type=F32) == own
        both = jnp.where(lane32 < 8, high, jnp.where(lane32 < 16, value - high, 0.0))
        send[6][k, rows32(y)] = jnp.where(match, both, 0.0).astype(BF16)
        h = h * w
        ag[k, y] = (h * u * s * (1.0 + g * (1.0 - s))).reshape(4, 8, 768)
        au[k, y] = (h * silu).reshape(4, 8, 768)
        return 0

    lax.fori_loop(0, 32, derive, 0)
    slot_start(1, send[6], vr, 0, 6)
    for p, (_, _, _, c0, cols) in enumerate(PARTS):
        ordered(ag, gb, p)
        ordered(au, ub, p)

        def backward(n0, width, p=p, c0=c0):
            at = pl.ds(c0 + n0, width)
            r = contract(gb[...], wg[at, :], 1, 1) + contract(ub[...], wu[at, :], 1, 1)
            send[3 + p][:, :, pl.ds(n0, width)] = r.astype(BF16).reshape(8, 128, width)

        tiles(cols, backward)
        slot_start(1, send[3 + p], cb[p], p, 3 + p)

    sent = []
    back_in = [*xb, *cb, vr]

    def go(copy):
        copy.start()
        sent.append(copy)

    def ring_copy(p, n, chunk, kind):
        a2 = PARTS[p][1]
        target = device(moved(co, a2, (co[a2] + (1 if kind in (0, 2, 3) else 3)) % 4), core)
        return remote(send[n].at[chunk], ring[n].at[kind], s5.at[n, kind], r5.at[n, kind], target)

    def ring_first(p, n):
        slot_sent(1, n)
        slot_got(1, n)
        cols = send[n].shape[-1]
        me = co[PARTS[p][1]]
        for d in (2, 1, 3, 0):
            g = (me + d) % 4
            got = back_in[n][:, pl.ds(pl.multiple_of(g * 32, 32), 32), :].reshape(256, cols)
            r = jnp.dot(st[p, g], got, preferred_element_type=F32)
            send[n][pl.ds(2 * g, 2)] = r.astype(BF16).reshape(2, 128, cols)
            if d == 2:
                go(ring_copy(p, n, 2 * g, 0))
                go(ring_copy(p, n, 2 * g + 1, 1))
            if d == 1:
                go(ring_copy(p, n, 2 * g + 1, 3))
            if d == 3:
                go(ring_copy(p, n, 2 * g, 4))

    def stage(i, cols):
        return hw[0].at[128 * i : 128 * i + 128, 0:cols]

    def ring_pass(items):
        todo = []
        for i, (p, n) in enumerate(items):
            me = co[PARTS[p][1]]
            cols = send[n].shape[-1]
            for j, (chunk, out) in enumerate(((2 * ((me + 1) % 4), 2), (2 * ((me + 3) % 4) + 1, 5))):
                ring_copy(p, n, chunk, j).wait_recv()
                slot = 2 * i + j
                copy = pltpu.make_async_copy(ring[n].at[j], stage(slot, cols), ls.at[slot])
                copy.start()
                todo.append((p, n, chunk, out, copy, stage(slot, cols)))
        for p, n, chunk, out, copy, held in todo:
            copy.wait()
            send[n][chunk] = (send[n][chunk].astype(F32) + held[...].astype(F32)).astype(BF16)
            go(ring_copy(p, n, chunk, out))

    def line_first(items):
        todo = []

        def finish(p, n, copies):
            a1, a2 = PARTS[p][:2]
            for h in (0, 1):
                chunk = 2 * co[a2] + h
                total = send[n][chunk].astype(F32)
                for copy, held in copies[h]:
                    copy.wait()
                    total = total + held[...].astype(F32)
                send[n][chunk] = total.astype(BF16)
            for d in (2, 1, 3):
                i = (co[a1] + d) % 4
                chunk, at = source(p, co[a2], i)
                go(remote(
                    send[n].at[chunk, at], line[n].at[co[a1]], s6.at[n, d - 1], r6.at[n, co[a1]],
                    device(moved(co, a1, i), core),
                ))
            chunk, at = source(p, co[a2], co[a1])
            mine = pltpu.make_async_copy(send[n].at[chunk, at], line[n].at[co[a1]], s6.at[n, 3])
            mine.start()
            owns.append(mine)

        for i, (p, n) in enumerate(items):
            cols = send[n].shape[-1]
            copies = ([], [])
            for kind in (2, 3, 4, 5):
                ring_copy(p, n, 0, kind).wait_recv()
                slot = 4 * (i % 2) + kind - 2
                copy = pltpu.make_async_copy(ring[n].at[kind], stage(slot, cols), ls.at[slot])
                copy.start()
                copies[kind % 2].append((copy, stage(slot, cols)))
            todo.append((p, n, copies))
            if i:
                finish(*todo[i - 1])
        finish(*todo[-1])

    owns = []
    outs = [(p, p) for p in range(3)]
    backs = [(0, 6)] + [(p, 3 + p) for p in range(3)]
    for item in outs:
        ring_first(*item)
    for p, (_, _, _, c0, cols) in enumerate(PARTS):

        def down(n, _, p=p, c0=c0, cols=cols):
            at = pl.ds(pl.multiple_of(n * 256, 256), 256)
            wd[at, c0 : c0 + cols] = contract(hw[p][:, at], c[p][...].reshape(1024, cols), 0, 0).astype(BF16)
            return 0

        lax.fori_loop(0, 3, down, 0)
    done = [pltpu.make_async_copy(wd, dgrad, sg.at[0])]
    done[0].start()
    ring_pass(outs)
    for item in backs:
        ring_first(*item)
    line_first(outs)

    def weight_grads(p):
        c0, cols = PARTS[p][3:]

        def gate(n0, width):
            part = x[p][:, :, pl.ds(n0, width)].reshape(1024, width)
            at = pl.ds(c0 + n0, width)
            wg[at, :] = contract(part, gb[...], 0, 0).astype(BF16)
            wu[at, :] = contract(part, ub[...], 0, 0).astype(BF16)

        tiles(cols, gate)
        for i, (src, dst) in enumerate(((wg, ggrad), (wu, ugrad))):
            copy = pltpu.make_async_copy(src.at[pl.ds(c0, cols)], dst.at[pl.ds(c0, cols)], sg.at[1 + 2 * p + i])
            copy.start()
            done.append(copy)

    weight_grads(2)
    ring_pass(backs)
    ordered(ag, gb, 1)
    ordered(au, ub, 1)
    weight_grads(1)
    line_first(backs)
    ordered(ag, gb, 0)
    ordered(au, ub, 0)
    weight_grads(0)
    for p, n in outs + backs:
        a1 = PARTS[p][0]
        for d in (1, 2, 3):
            j = (co[a1] + d) % 4
            got = line[n].at[j]
            remote(got, got, s6.at[n, d - 1], r6.at[n, j], device(moved(co, a1, j), core)).wait_recv()
    for copy in sent:
        copy.wait_send()
    for copy in owns + done:
        copy.wait()


def last_kernel(*refs):
    line, grads, outs = refs[0:7], refs[7:10], refs[10:16]
    held, mixed, tgrad, vgrad = refs[16:20]
    kept, (ls, gs, hs, os) = refs[20:23], refs[23:27]
    pieces_of = []
    for i in range(3):
        part = grads[i].shape[0] // 4
        for j in range(4):
            at = pl.ds(j * part, part)
            pieces_of.append((
                pltpu.make_async_copy(grads[i].at[at], kept[i].at[at], gs.at[i, j]),
                pltpu.make_async_copy(kept[i].at[at], outs[3 + i].at[at], hs.at[i, j]),
            ))
    spans = [(c0, cols) for _, _, _, c0, cols in PARTS]
    places = [(0, *span) for span in spans] + [(1, *span) for span in spans] + [(2, 0, 128)]
    loads = [
        pltpu.make_async_copy(line[n], held.at[a, :, :, pl.ds(c0, cols)], ls.at[n])
        for n, (a, c0, cols) in enumerate(places)
    ]
    for load in loads + [first for first, _ in pieces_of]:
        load.start()
    for first, second in pieces_of:
        first.wait()
        second.start()
    for load in loads:
        load.wait()

    def total(a, at):
        return jnp.sum(held[a, :, at, :].astype(F32), axis=0)

    def step(i, _):
        at = pl.ds(pl.multiple_of(i * 16, 16), 16)
        mixed[at, :] = total(0, at).astype(BF16)
        tgrad[at, :] = total(1, at).astype(BF16)
        return 0

    lax.fori_loop(0, 4, step, 0)
    lane = lax.broadcasted_iota(jnp.int32, (8, 128), 1)
    row = lax.broadcasted_iota(jnp.int32, (8, 128), 0)
    both = jnp.where((lane < 16) & (lane % 8 == row), 1.0, 0.0).astype(BF16)
    value = jnp.sum(held[2, :, :, 0:128].astype(F32), axis=0).astype(BF16)
    vgrad[...] = contract(both, value, 1, 1)
    ends = [pltpu.make_async_copy(src, dst, os.at[i]) for i, (src, dst) in enumerate(zip((mixed, tgrad, vgrad), outs[:3], strict=True))]
    for copy in ends:
        copy.start()
    for copy in ends + [second for _, second in pieces_of]:
        copy.wait()


def per_device(tokens, routes, route_weights, cotangent, gate_weight, up_weight, down_weight):
    widths = [part[4] for part in PARTS]
    shape, dma = jax.ShapeDtypeStruct, pltpu.SemaphoreType.DMA
    any_, vmem = pl.BlockSpec(memory_space=pl.ANY), pl.BlockSpec(memory_space=pltpu.VMEM)
    items = widths * 2 + [128]
    weight_shapes = [shape((2048, 768), BF16), shape((2048, 768), BF16), shape((768, 2048), BF16)]

    def chunks(ws):
        return [pltpu.VMEM((8, 128, w), BF16) for w in ws]

    got = pl.pallas_call(
        moe_kernel,
        out_shape=weight_shapes + [shape((6, 128, w), BF16) for w in items] + [shape((4, 64, w), BF16) for w in items],
        in_specs=[vmem] * 4 + [any_] * 3,
        out_specs=[any_] * 17,
        scratch_shapes=chunks(widths * 2 + [128] * 5)
        + chunks(items)
        + chunks(items)
        + [pltpu.VMEM((3, 4, 256, 256), BF16)]
        + [pltpu.VMEM((2048, 768), BF16), pltpu.VMEM((2048, 768), BF16), pltpu.VMEM((768, 2048), BF16)]
        + [pltpu.VMEM((8, 4, 4, 8, 768), F32)] * 3
        + [pltpu.VMEM((1024, 768), BF16)] * 5
        + [pltpu.VMEM((8, 128, 128), F32)]
        + [dma((10, 3)), dma((10, 4)), dma((10, 6)), dma((10, 4, 2)), dma((7, 8)), dma((7, 8)), dma((7,)), dma((3,))]
        + [dma((7, 8)), dma((7, 8)), dma((7,)), dma((7, 6)), dma((7, 6)), dma((7, 4)), dma((7, 4)), dma((7,)), dma((8,))],
        compiler_params=pltpu.CompilerParams(collective_id=0, has_side_effects=True, vmem_limit_bytes=62 * 2**20),
    )(tokens, cotangent, routes.T, route_weights.T, gate_weight[0], up_weight[0], down_weight[0])
    mixed, token_grad, weight_grad, gate_grad, up_grad, down_grad = pl.pallas_call(
        last_kernel,
        out_shape=[shape((64, 2048), BF16), shape((64, 2048), BF16), shape((8, 64), F32)] + weight_shapes,
        in_specs=[any_] * 10,
        out_specs=[any_] * 6,
        scratch_shapes=[
            pltpu.VMEM((3, 4, 64, 2048), BF16),
            pltpu.VMEM((64, 2048), BF16),
            pltpu.VMEM((64, 2048), BF16),
            pltpu.VMEM((8, 64), F32),
            *[pltpu.VMEM(w.shape, BF16) for w in weight_shapes],
            dma((7,)),
            dma((3, 4)),
            dma((3, 4)),
            dma((3,)),
        ],
        compiler_params=pltpu.CompilerParams(vmem_limit_bytes=61 * 2**20),
    )(*got[10:17], *got[0:3])
    return (mixed, token_grad, weight_grad.T, gate_grad[None], up_grad[None], down_grad[None])


def solution(mesh):
    placed = (
        P(("node", "rail"), None),
        P(("node", "rail"), None),
        P(("node", "rail"), None),
        P(("node", "rail"), None),
        P(("node", "rail"), None, None),
        P(("node", "rail"), None, None),
        P(("node", "rail"), None, None),
    )
    return jax.shard_map(
        per_device,
        mesh=mesh,
        in_specs=placed,
        out_specs=(
            P(("node", "rail"), None),
            P(("node", "rail"), None),
            P(("node", "rail"), None),
            P(("node", "rail"), None, None),
            P(("node", "rail"), None, None),
            P(("node", "rail"), None, None),
        ),
        check_vma=False,
    )
```

time: 290 us -> 181 us (0.62); the launches traced: 285 us -> 180 us
  Pallas kernels: 0 us -> 179 us
  waiting for transfers between devices: 130 us -> 0 us
  matrix products: 66.1 us -> 0 us
  local copies, waits for them, and re-layouts: 44.6 us -> 0 us
  starting transfers between devices: 28 us -> 0 us
  other arithmetic: 14.7 us -> 0 us
    pallas_call x0 -> x2, Pallas kernels: none -> 179 us  [the longest x1 171 us: per_device(): pl.pallas_call(moe_kernel, out_shape=weight_shapes + [shape((6, 128, w),...]
    all_to_all x4 -> x0, waiting for transfers between devices: 130 us -> none  [the longest x1 41.9 us: per_device(): lax.all_to_all(output.reshape(experts, capacity, model_width), ('node', '...]
    dot_general x11 -> x0, matrix products: 66.1 us -> none  [the longest x1 10.2 us: expert_backward(): lax.dot_general(slot_grads, w_down, contract_last, preferred_element_type...]
    gather x5 -> x0, local copies, waits for them, and re-layouts: 34.4 us -> none  [the longest x1 8.16 us: per_device(): back_home.reshape(-1, model_width)[slot_index]]
    all_to_all x4 -> x0, starting transfers between devices: 28 us -> none  [the longest x1 11.2 us: per_device(): lax.all_to_all(send_rows, ('node', 'rail'), split_axis=0, concat_axis=0,...]
    scatter x2 -> x0, local copies, waits for them, and re-layouts: 4.89 us -> none  [the longest x1 2.45 us: per_device(): owner_row = jnp.zeros((total_slots,), jnp.int32).at[slot_index].set(jnp.a...]
    select_n x2 -> x0, other arithmetic: 4.54 us -> none  [the longest x1 4.53 us: per_device(): jnp.where(keep_mask, tokens[token_of], jnp.zeros((), jnp.bfloat16))]
    convert_element_type x1 -> x0, other arithmetic: 4.1 us -> none  [per_device(): send_grads = jnp.where(keep_mask, weight_of[:, None] * cotangent[token_of...]
  transfers between devices with their start and end apart: 4 -> 0, of which waited for: 4 -> 0; matrix products, arithmetic and copies ran while one was open for 27% -> 0% of each run, Pallas kernels for 0% -> 0%
where the time goes in v3:
time: 181 us; the launch traced here: 180 us
  Pallas kernels  179 us (99%)
    pallas_call x1, Pallas kernels, per_device(): pl.pallas_call(moe_kernel, out_shape=weight_shapes + [shape((6, 128, w),...  171 us
    pallas_call x1, Pallas kernels, per_device(): pl.pallas_call(last_kernel, out_shape=[shape((64, 2048), BF16), shape((64...  8.51 us

profile of v3, /device:TPU:7, one launch (start us, length us, event | category | flops | bytes accessed | tf_op | source)
XLA Modules:
  0.0 180.1 jit_solution(9263030798581806135)
XLA Ops:
  0.6 170.8 %shard_map.118 = (bf16[2048,768]{1,0:T(8,128)(2,1)}, bf16[2048,768]{1,0:T(8,128)(2,1)}, bf16[768,2048]{1,0:T(8,128)(2,1)}, bf16[6,128,768]{2,1,0:T(8,128)(2,1)},...) custom-call(bf16[64,2048]{1,0:T(8,128)(2,1)} %tok.1, ...), custom_call_target="tpu_custom_call" | custom-call | tf_op jit(solution)/shard_map/pallas_call | solution.py:591
  171.4 8.5 %shard_map.119 = (bf16[64,2048]{1,0:T(8,128)(2,1)}, bf16[64,2048]{1,0:T(8,128)(2,1)}, f32[8,64]{1,0:T(8,128)}, bf16[2048,768]{1,0:T(8,128)(2,1)}, bf16[2048,768]{1,0:T(8,128)(2,1)}, /*index=5*/bf16[768,2048]{1,0:T(8,128)(2,1)}) custom-call(bf16[4,64,768]{2,1,0:T(8,128)(2,1)} %get-tuple-element.22.refs_0_, bf16[4,64,640]{2,1,0:T(8,128)(2,1)} %get-tuple-element.23.refs_1_, ...), custom_call_target="tpu_custom_call" | custom-call | tf_op jit(solution)/shard_map/pallas_call | solution.py:608

commit v4 on v3

--- a/solution.py
+++ b/solution.py
@@ -104,16 +104,15 @@
 
 
 def moe_kernel(tok, cot, routes, weights, wgi, wui, wdi, *refs):
-    ggrad, ugrad, dgrad = refs[0:3]
+    wg, wu, wd = refs[0:3]
     ring, line = refs[3:10], refs[10:17]
     refs = refs[17:]
     xb, cb, vr, qb, rwb = refs[0:3], refs[3:6], refs[6], refs[7:10], refs[10]
     send = refs[11:18]
     x, c, rw, st = refs[18:21], refs[21:24], refs[24], refs[25]
-    wg, wu, wd = refs[26:29]
-    ag, au, ah = refs[29:32]
-    hw, gb, ub, wcol = refs[32:35], refs[35], refs[36], refs[37]
-    s1, r1, s2, r2, s3, r3, loc3, ld, s4, r4, loc4, s5, r5, s6, r6, sg, ls = refs[38:55]
+    ag, au, ah = refs[26:29]
+    hw, gb, ub, wcol, rep = refs[29:32], refs[32], refs[33], refs[34], refs[35]
+    s1, r1, s2, r2, s3, r3, loc3, ld, s4, r4, loc4, s5, r5, s6, r6, ls = refs[36:52]
     co, core = place()
     own = ((co[0] * 2 + core) * 16 + co[2] * 4 + co[1] + 1).astype(F32)
     barrier, count = greet(co, core)
@@ -127,7 +126,7 @@
 
     rows = [(xb[p], p, p) for p in range(3)]
     grads = [(cb[p], p, 3 + p) for p in range(3)]
-    tables = [(qb[p], p, 6 + p) for p in range(3)] + [(rwb, 0, 9)]
+    tables = [(qb[p], p, 6 + p) for p in range(3)] + [(rwb, 1, 9)]
 
     def put(buf, p, value):
         a1, a2 = PARTS[p][:2]
@@ -199,7 +198,7 @@
     table, extra = route_tables(routes[...], weights[...])
     for p in range(3):
         put(qb[p], p, table)
-    put(rwb, 0, extra)
+    put(rwb, 1, extra)
     for item in tables:
         first_start(*item)
     for p, (_, _, _, c0, cols) in enumerate(PARTS):
@@ -211,7 +210,7 @@
     for item in rows + tables + grads:
         first_wait(*item)
         second_start(*item)
-    for item in tables + rows:
+    for item in rows + tables + grads:
         relay(*item)
     for item in tables:
         rest_wait(*item)
@@ -264,15 +263,13 @@
         for i, k, to in slot_ends(p):
             remote(src.at[k], dst.at[k], ss.at[n, i], rs.at[n, k], to).wait_recv()
 
-    pick(rwb, send[6], 0)
-    slot_start(0, send[6], rw, 0, 6)
+    pick(rwb, send[6], 1)
+    slot_start(0, send[6], rw, 1, 6)
     for p in range(3):
         rest_wait(*rows[p])
         pick(xb[p], send[p], p)
         landed(p)
         slot_start(0, send[p], x[p], p, p)
-    for item in grads:
-        relay(*item)
     for p in range(3):
         rest_wait(*grads[p])
         pick(cb[p], send[3 + p], p)
@@ -308,22 +305,24 @@
     row = lax.broadcasted_iota(jnp.int32, (128, 128), 0)
     spread = jnp.where((row < 8) & (lane < 32) & (lane % 8 == row), 1.0, 0.0).astype(BF16)
 
-    def weigh(k, _):
-        route = jnp.dot(rw[k], spread, preferred_element_type=F32)
-        taken = jnp.where((route == own) & (lane >= 8), rw[k].astype(F32), 0.0)
-        wcol[k] = jnp.broadcast_to(jnp.sum(taken, axis=1, keepdims=True), (128, 128))
-        return 0
-
-    lax.fori_loop(0, 8, weigh, 0)
-
-    def rows32(y):
-        return pl.ds(pl.multiple_of(y * 32, 32), 32)
+    for start, count, at in pieces(1):
+        extra = rw[start // 128]
+        route = jnp.dot(extra, spread, preferred_element_type=F32)
+        taken = jnp.where((route == own) & (lane >= 8), extra.astype(F32), 0.0)
+        wcol[at] = jnp.broadcast_to(jnp.sum(taken, axis=1, keepdims=True), (128, 128)).reshape(4, 4, 8, 128)
+        rep[at] = route.reshape(4, 4, 8, 128)
 
     def activate(i, _):
         k, y = i // 4, i % 4
         g, u = ag[k, y].reshape(32, 768), au[k, y].reshape(32, 768)
-        w = wcol[k, rows32(y), 0:1]
-        ah[k, y] = (g * jax.nn.sigmoid(g) * u * w).reshape(4, 8, 768)
+        w = wcol[k, y].reshape(32, 128)[:, 0:1]
+        s = jax.nn.sigmoid(g)
+        silu = g * s * w
+        hidden = silu * u
+        ah[k, y] = hidden.reshape(4, 8, 768)
+        hw[0][pl.ds(pl.multiple_of(i * 32, 32), 32), :] = hidden.astype(BF16)
+        ag[k, y] = (u * s * w * (1.0 + g * (1.0 - s))).reshape(4, 8, 768)
+        au[k, y] = silu.reshape(4, 8, 768)
         return 0
 
     lax.fori_loop(0, 32, activate, 0)
@@ -333,7 +332,8 @@
             out[row : row + count, :] = acc[at].reshape(count, 768).astype(BF16)
 
     for p, (_, _, _, c0, cols) in enumerate(PARTS):
-        ordered(ah, hw[p], p)
+        if p:
+            ordered(ah, hw[p], p)
 
         def forward(n0, width, p=p, c0=c0):
             r = jnp.dot(hw[p][...], wd[:, pl.ds(c0 + n0, width)], preferred_element_type=F32)
@@ -358,25 +358,26 @@
 
     def derive(i, _):
         k, y = i // 4, i % 4
-        g, u, h = ag[k, y].reshape(32, 768), au[k, y].reshape(32, 768), ah[k, y].reshape(32, 768)
-        w = wcol[k, rows32(y), 0:1]
-        s = jax.nn.sigmoid(g)
-        silu = g * s
-        value = jnp.sum(silu * u * h, axis=1, keepdims=True)
+        at = pl.ds(pl.multiple_of(i * 32, 32), 32)
+        h = ah[k, y].reshape(32, 768)
+        gate, up = h * ag[k, y].reshape(32, 768), h * au[k, y].reshape(32, 768)
+        ag[k, y], au[k, y] = gate.reshape(4, 8, 768), up.reshape(4, 8, 768)
+        gb[at, :], ub[at, :] = gate.astype(BF16), up.astype(BF16)
+        w = wcol[k, y].reshape(32, 128)
+        value = jnp.sum(hw[0][at, :].astype(F32) * h, axis=1, keepdims=True) / w
         high = value.astype(BF16).astype(F32)
-        match = jnp.dot(rw[k, rows32(y)], spread, preferred_element_type=F32) == own
         both = jnp.where(lane32 < 8, high, jnp.where(lane32 < 16, value - high, 0.0))
-        send[6][k, rows32(y)] = jnp.where(match, both, 0.0).astype(BF16)
-        h = h * w
-        ag[k, y] = (h * u * s * (1.0 + g * (1.0 - s))).reshape(4, 8, 768)
-        au[k, y] = (h * silu).reshape(4, 8, 768)
+        rep[k, y] = jnp.where(rep[k, y].reshape(32, 128) == own, both, 0.0).reshape(4, 8, 128)
         return 0
 
     lax.fori_loop(0, 32, derive, 0)
-    slot_start(1, send[6], vr, 0, 6)
+    for start, count, at in pieces(1):
+        send[6][start // 128] = rep[at].reshape(128, 128).astype(BF16)
+    slot_start(1, send[6], vr, 1, 6)
     for p, (_, _, _, c0, cols) in enumerate(PARTS):
-        ordered(ag, gb, p)
-        ordered(au, ub, p)
+        if p:
+            ordered(ag, gb, p)
+            ordered(au, ub, p)
 
         def backward(n0, width, p=p, c0=c0):
             at = pl.ds(c0 + n0, width)
@@ -475,7 +476,7 @@
 
     owns = []
     outs = [(p, p) for p in range(3)]
-    backs = [(0, 6)] + [(p, 3 + p) for p in range(3)]
+    backs = [(1, 6)] + [(p, 3 + p) for p in range(3)]
     for item in outs:
         ring_first(*item)
     for p, (_, _, _, c0, cols) in enumerate(PARTS):
@@ -486,12 +487,6 @@
             return 0
 
         lax.fori_loop(0, 3, down, 0)
-    done = [pltpu.make_async_copy(wd, dgrad, sg.at[0])]
-    done[0].start()
-    ring_pass(outs)
-    for item in backs:
-        ring_first(*item)
-    line_first(outs)
 
     def weight_grads(p):
         c0, cols = PARTS[p][3:]
@@ -503,20 +498,20 @@
             wu[at, :] = contract(part, ub[...], 0, 0).astype(BF16)
 
         tiles(cols, gate)
-        for i, (src, dst) in enumerate(((wg, ggrad), (wu, ugrad))):
-            copy = pltpu.make_async_copy(src.at[pl.ds(c0, cols)], dst.at[pl.ds(c0, cols)], sg.at[1 + 2 * p + i])
-            copy.start()
-            done.append(copy)
 
     weight_grads(2)
-    ring_pass(backs)
+    for item in backs:
+        ring_first(*item)
     ordered(ag, gb, 1)
     ordered(au, ub, 1)
     weight_grads(1)
-    line_first(backs)
+    ring_pass(outs)
     ordered(ag, gb, 0)
     ordered(au, ub, 0)
     weight_grads(0)
+    ring_pass(backs)
+    line_first(outs)
+    line_first(backs)
     for p, n in outs + backs:
         a1 = PARTS[p][0]
         for d in (1, 2, 3):
@@ -525,34 +520,28 @@
             remote(got, got, s6.at[n, d - 1], r6.at[n, j], device(moved(co, a1, j), core)).wait_recv()
     for copy in sent:
         copy.wait_send()
-    for copy in owns + done:
+    for copy in owns:
         copy.wait()
 
 
 def last_kernel(*refs):
     line, grads, outs = refs[0:7], refs[7:10], refs[10:16]
     held, mixed, tgrad, vgrad = refs[16:20]
-    kept, (ls, gs, hs, os) = refs[20:23], refs[23:27]
-    pieces_of = []
+    ls, hs, os = refs[20:23]
+    copies = []
     for i in range(3):
         part = grads[i].shape[0] // 4
         for j in range(4):
             at = pl.ds(j * part, part)
-            pieces_of.append((
-                pltpu.make_async_copy(grads[i].at[at], kept[i].at[at], gs.at[i, j]),
-                pltpu.make_async_copy(kept[i].at[at], outs[3 + i].at[at], hs.at[i, j]),
-            ))
+            copies.append(pltpu.make_async_copy(grads[i].at[at], outs[3 + i].at[at], hs.at[i, j]))
     spans = [(c0, cols) for _, _, _, c0, cols in PARTS]
     places = [(0, *span) for span in spans] + [(1, *span) for span in spans] + [(2, 0, 128)]
     loads = [
         pltpu.make_async_copy(line[n], held.at[a, :, :, pl.ds(c0, cols)], ls.at[n])
         for n, (a, c0, cols) in enumerate(places)
     ]
-    for load in loads + [first for first, _ in pieces_of]:
+    for load in loads + copies:
         load.start()
-    for first, second in pieces_of:
-        first.wait()
-        second.start()
     for load in loads:
         load.wait()
 
@@ -574,7 +563,7 @@
     ends = [pltpu.make_async_copy(src, dst, os.at[i]) for i, (src, dst) in enumerate(zip((mixed, tgrad, vgrad), outs[:3], strict=True))]
     for copy in ends:
         copy.start()
-    for copy in ends + [second for _, second in pieces_of]:
+    for copy in ends + copies:
         copy.wait()
 
 
@@ -590,20 +579,19 @@
 
     got = pl.pallas_call(
         moe_kernel,
-        out_shape=weight_shapes + [shape((6, 128, w), BF16) for w in items] + [shape((4, 64, w), BF16) for w in items],
+        out_shape=[pltpu.VMEM(w.shape, BF16) for w in weight_shapes] + [shape((6, 128, w), BF16) for w in items] + [shape((4, 64, w), BF16) for w in items],
         in_specs=[vmem] * 4 + [any_] * 3,
-        out_specs=[any_] * 17,
+        out_specs=[vmem] * 3 + [any_] * 14,
         scratch_shapes=chunks(widths * 2 + [128] * 5)
         + chunks(items)
         + chunks(items)
         + [pltpu.VMEM((3, 4, 256, 256), BF16)]
-        + [pltpu.VMEM((2048, 768), BF16), pltpu.VMEM((2048, 768), BF16), pltpu.VMEM((768, 2048), BF16)]
         + [pltpu.VMEM((8, 4, 4, 8, 768), F32)] * 3
         + [pltpu.VMEM((1024, 768), BF16)] * 5
-        + [pltpu.VMEM((8, 128, 128), F32)]
+        + [pltpu.VMEM((8, 4, 4, 8, 128), F32)] * 2
         + [dma((10, 3)), dma((10, 4)), dma((10, 6)), dma((10, 4, 2)), dma((7, 8)), dma((7, 8)), dma((7,)), dma((3,))]
-        + [dma((7, 8)), dma((7, 8)), dma((7,)), dma((7, 6)), dma((7, 6)), dma((7, 4)), dma((7, 4)), dma((7,)), dma((8,))],
-        compiler_params=pltpu.CompilerParams(collective_id=0, has_side_effects=True, vmem_limit_bytes=62 * 2**20),
+        + [dma((7, 8)), dma((7, 8)), dma((7,)), dma((7, 6)), dma((7, 6)), dma((7, 4)), dma((7, 4)), dma((8,))],
+        compiler_params=pltpu.CompilerParams(collective_id=0, has_side_effects=True, vmem_limit_bytes=53 * 2**20),
     )(tokens, cotangent, routes.T, route_weights.T, gate_weight[0], up_weight[0], down_weight[0])
     mixed, token_grad, weight_grad, gate_grad, up_grad, down_grad = pl.pallas_call(
         last_kernel,
@@ -615,14 +603,12 @@
             pltpu.VMEM((64, 2048), BF16),
             pltpu.VMEM((64, 2048), BF16),
             pltpu.VMEM((8, 64), F32),
-            *[pltpu.VMEM(w.shape, BF16) for w in weight_shapes],
             dma((7,)),
-            dma((3, 4)),
             dma((3, 4)),
             dma((3,)),
         ],
-        compiler_params=pltpu.CompilerParams(vmem_limit_bytes=61 * 2**20),
-    )(*got[10:17], *got[0:3])
+        compiler_params=pltpu.CompilerParams(vmem_limit_bytes=16 * 2**20),
+    )(*[pltpu.with_memory_space_constraint(g, pltpu.HBM) for g in got[10:17]], *[pltpu.with_memory_space_constraint(g, pltpu.VMEM) for g in got[0:3]])
     return (mixed, token_grad, weight_grad.T, gate_grad[None], up_grad[None], down_grad[None])
 
 

time: 181 us -> 166 us (0.917)
  Pallas kernels: 179 us -> 163 us
    pallas_call x1, Pallas kernels: 171 us -> 158 us  [per_device(): pl.pallas_call(moe_kernel, out_shape=[pltpu.VMEM(w.shape, BF16) for w in...]
    pallas_call x1, Pallas kernels: 8.51 us -> 4.31 us  [per_device(): pl.pallas_call(last_kernel, out_shape=[shape((64, 2048), BF16), shape((64...]
where the time goes in v4:
time: 166 us; the launch traced here: 163 us
  Pallas kernels  163 us (98%)
    pallas_call x1, Pallas kernels, per_device(): pl.pallas_call(moe_kernel, out_shape=[pltpu.VMEM(w.shape, BF16) for w in...  158 us
    pallas_call x1, Pallas kernels, per_device(): pl.pallas_call(last_kernel, out_shape=[shape((64, 2048), BF16), shape((64...  4.31 us

profile of v4, /device:TPU:7, one launch (start us, length us, event | category | flops | bytes accessed | tf_op | source)
XLA Modules:
  0.0 163.4 jit_solution(8927613492674738351)
XLA Ops:
  0.6 158.2 %shard_map.118 = (bf16[2048,768]{1,0:T(8,128)(2,1)S(1)}, bf16[2048,768]{1,0:T(8,128)(2,1)S(1)}, bf16[768,2048]{1,0:T(8,128)(2,1)S(1)}, bf16[6,128,768]{2,1,0:T(8...) custom-call(bf16[64,2048]{1,0:T(8,128)(2,1)} %tok.1, ...), custom_call_target="tpu_custom_call" | custom-call | tf_op jit(solution)/shard_map/pallas_call | solution.py:580
  158.9 4.3 %shard_map.119 = (bf16[64,2048]{1,0:T(8,128)(2,1)}, bf16[64,2048]{1,0:T(8,128)(2,1)}, f32[8,64]{1,0:T(8,128)}, bf16[2048,768]{1,0:T(8,128)(2,1)}, bf16[2048,768]{1,0:T(8,128)(2,1)}, /*index=5*/bf16[768,2048]{1,0:T(8,128)(2,1)}) custom-call(bf16[4,64,768]{2,1,0:T(8,128)(2,1)} %get-tuple-element.22.refs_0_, bf16[4,64,640]{2,1,0:T(8,128)(2,1)} %get-tuple-element.23.refs_1_, ...), custom_call_target="tpu_custom_call" | custom-call | tf_op jit(solution)/shard_map/pallas_call | solution.py:596

commit v5 on v4

--- a/solution.py
+++ b/solution.py
@@ -186,9 +186,23 @@
         second_wait(buf, p, n, 1, 1)
         launch(n, [second_copy(buf, p, n, (me + 1) % 4, 1, False, 5)])
 
-    def rest_wait(buf, p, n):
-        for d, h in ((3, 1), (1, 0), (2, 0), (2, 1)):
-            second_wait(buf, p, n, d, h)
+    def near_wait(buf, p, n):
+        second_wait(buf, p, n, 3, 1)
+        second_wait(buf, p, n, 1, 0)
+
+    def far_wait(buf, p, n):
+        second_wait(buf, p, n, 2, 0)
+        second_wait(buf, p, n, 2, 1)
+
+    def build(p, d):
+        g = (co[PARTS[p][1]] + d) % 4
+        st[p, g] = one_hot(qb[p][pl.ds(2 * g, 2)].reshape(256, 128), co, PARTS[p][2])
+
+    def pick(buf, out, p, d):
+        cols = buf.shape[-1]
+        g = (co[PARTS[p][1]] + d) % 4
+        r = contract(st[p, g], buf[pl.ds(2 * g, 2)].reshape(256, cols), 0, 0)
+        out[:, pl.ds(pl.multiple_of(g * 32, 32), 32), :] = r.astype(BF16).reshape(8, 32, cols)
 
     for p, (_, _, _, c0, cols) in enumerate(PARTS):
         put(xb[p], p, tok[:, c0 : c0 + cols])
@@ -210,28 +224,6 @@
     for item in rows + tables + grads:
         first_wait(*item)
         second_start(*item)
-    for item in rows + tables + grads:
-        relay(*item)
-    for item in tables:
-        rest_wait(*item)
-    for p, (_, _, slot_axis, _, _) in enumerate(PARTS):
-
-        def build(g, _, p=p, slot_axis=slot_axis):
-            st[p, g] = one_hot(qb[p][pl.ds(2 * g, 2)].reshape(256, 128), co, slot_axis)
-            return 0
-
-        lax.fori_loop(0, 4, build, 0)
-
-    def pick(buf, out, p):
-        cols = buf.shape[-1]
-
-        def step(g, _):
-            r = contract(st[p, g], buf[pl.ds(2 * g, 2)].reshape(256, cols), 0, 0)
-            out[:, pl.ds(pl.multiple_of(g * 32, 32), 32), :] = r.astype(BF16).reshape(8, 32, cols)
-            return 0
-
-        lax.fori_loop(0, 4, step, 0)
-
     def slot_ends(p):
         axis = PARTS[p][2]
         for dc in (0, 1):
@@ -263,24 +255,47 @@
         for i, k, to in slot_ends(p):
             remote(src.at[k], dst.at[k], ss.at[n, i], rs.at[n, k], to).wait_recv()
 
-    pick(rwb, send[6], 1)
-    slot_start(0, send[6], rw, 1, 6)
-    for p in range(3):
-        rest_wait(*rows[p])
-        pick(xb[p], send[p], p)
+    for p in range(3):
+        build(p, 0)
+    pick(rwb, send[6], 1, 0)
+    for p in range(3):
+        pick(xb[p], send[p], p, 0)
+    for item in rows + tables + grads:
+        relay(*item)
+    for item in tables:
+        near_wait(*item)
+    for p in range(3):
+        build(p, 1)
+        build(p, 3)
+    for p in range(3):
+        near_wait(*rows[p])
+        pick(xb[p], send[p], p, 1)
+        pick(xb[p], send[p], p, 3)
+    pick(rwb, send[6], 1, 1)
+    pick(rwb, send[6], 1, 3)
+    for item in tables:
+        far_wait(*item)
+    for p in range(3):
+        build(p, 2)
+    for p in range(3):
+        far_wait(*rows[p])
+        pick(xb[p], send[p], p, 2)
         landed(p)
         slot_start(0, send[p], x[p], p, p)
-    for p in range(3):
-        rest_wait(*grads[p])
-        pick(cb[p], send[3 + p], p)
+    pick(rwb, send[6], 1, 2)
+    slot_start(0, send[6], rw, 1, 6)
+    for p in range(3):
+        near_wait(*grads[p])
+        for d in (0, 1, 3):
+            pick(cb[p], send[3 + p], p, d)
+    for p in range(3):
+        far_wait(*grads[p])
+        pick(cb[p], send[3 + p], p, 2)
         landed(3 + p)
         slot_start(0, send[3 + p], c[p], p, 3 + p)
     for n in range(6, 10):
         landed(n)
 
-    for n in (6, 0, 1, 2):
-        slot_sent(0, n)
-        slot_got(0, n)
     for load in loads:
         load.wait()
 
@@ -289,17 +304,23 @@
             at = (*at, *([slice(None)] * (4 - len(at))), pl.ds(n0, 256))
             where = acc.at[at]
             piece = r[row : row + count].reshape(where.shape)
-            where[...] = piece if p == 0 else where[...] + piece
-
-    def pre(n, _):
-        n0 = pl.multiple_of(n * 256, 256)
-        for w, acc in ((wg, ag), (wu, au)):
-            for p, (_, _, _, c0, cols) in enumerate(PARTS):
+            where[...] = piece if p == 2 else where[...] + piece
+
+    for p in (2, 1, 0):
+        c0, cols = PARTS[p][3:]
+        slot_sent(0, p)
+        slot_got(0, p)
+
+        def pre(n, _, p=p, c0=c0, cols=cols):
+            n0 = pl.multiple_of(n * 256, 256)
+            for w, acc in ((wg, ag), (wu, au)):
                 part = x[p][...].reshape(1024, cols)
                 gather_into(acc, jnp.dot(part, w[c0 : c0 + cols, pl.ds(n0, 256)], preferred_element_type=F32), p, n0)
-        return 0
-
-    lax.fori_loop(0, 3, pre, 0)
+            return 0
+
+        lax.fori_loop(0, 3, pre, 0)
+    slot_sent(0, 6)
+    slot_got(0, 6)
 
     lane = lax.broadcasted_iota(jnp.int32, (128, 128), 1)
     row = lax.broadcasted_iota(jnp.int32, (128, 128), 0)
@@ -342,18 +363,18 @@
         tiles(cols, forward)
         slot_start(1, send[p], xb[p], p, p)
 
-    for n in (3, 4, 5):
-        slot_sent(0, n)
-        slot_got(0, n)
-
-    def hidden_back(n, _):
-        n0 = pl.multiple_of(n * 256, 256)
-        for p, (_, _, _, c0, cols) in enumerate(PARTS):
+    for p in (2, 1, 0):
+        c0, cols = PARTS[p][3:]
+        slot_sent(0, 3 + p)
+        slot_got(0, 3 + p)
+
+        def hidden_back(n, _, p=p, c0=c0, cols=cols):
+            n0 = pl.multiple_of(n * 256, 256)
             r = contract(c[p][...].reshape(1024, cols), wd[pl.ds(n0, 256), c0 : c0 + cols], 1, 1)
             gather_into(ah, r, p, n0)
-        return 0
-
-    lax.fori_loop(0, 3, hidden_back, 0)
+            return 0
+
+        lax.fori_loop(0, 3, hidden_back, 0)
     lane32 = lax.broadcasted_iota(jnp.int32, (32, 128), 1)
 
     def derive(i, _):

time: 166 us -> 162 us (0.976)
  Pallas kernels: 163 us -> 159 us
    pallas_call x1, Pallas kernels: 158 us -> 155 us  [per_device(): pl.pallas_call(moe_kernel, out_shape=[pltpu.VMEM(w.shape, BF16) for w in...]
where the time goes in v5:
time: 162 us; the launch traced here: 160 us
  Pallas kernels  159 us (98%)
    pallas_call x1, Pallas kernels, per_device(): pl.pallas_call(moe_kernel, out_shape=[pltpu.VMEM(w.shape, BF16) for w in...  155 us
    pallas_call x1, Pallas kernels, per_device(): pl.pallas_call(last_kernel, out_shape=[shape((64, 2048), BF16), shape((64...  4.31 us

profile of v5, /device:TPU:7, one launch (start us, length us, event | category | flops | bytes accessed | tf_op | source)
XLA Modules:
  0.0 160.0 jit_solution(3978620348064692556)
XLA Ops:
  0.6 154.9 %shard_map.118 = (bf16[2048,768]{1,0:T(8,128)(2,1)S(1)}, bf16[2048,768]{1,0:T(8,128)(2,1)S(1)}, bf16[768,2048]{1,0:T(8,128)(2,1)S(1)}, bf16[6,128,768]{2,1,0:T(8...) custom-call(bf16[64,2048]{1,0:T(8,128)(2,1)} %tok.1, ...), custom_call_target="tpu_custom_call" | custom-call | tf_op jit(solution)/shard_map/pallas_call | solution.py:601
  155.5 4.3 %shard_map.119 = (bf16[64,2048]{1,0:T(8,128)(2,1)}, bf16[64,2048]{1,0:T(8,128)(2,1)}, f32[8,64]{1,0:T(8,128)}, bf16[2048,768]{1,0:T(8,128)(2,1)}, bf16[2048,768]{1,0:T(8,128)(2,1)}, /*index=5*/bf16[768,2048]{1,0:T(8,128)(2,1)}) custom-call(bf16[4,64,768]{2,1,0:T(8,128)(2,1)} %get-tuple-element.22.refs_0_, bf16[4,64,640]{2,1,0:T(8,128)(2,1)} %get-tuple-element.23.refs_1_, ...), custom_call_target="tpu_custom_call" | custom-call | tf_op jit(solution)/shard_map/pallas_call | solution.py:617

commit v6 on v5

--- a/solution.py
+++ b/solution.py
@@ -521,11 +521,11 @@
         tiles(cols, gate)
 
     weight_grads(2)
-    for item in backs:
-        ring_first(*item)
     ordered(ag, gb, 1)
     ordered(au, ub, 1)
     weight_grads(1)
+    for item in backs:
+        ring_first(*item)
     ring_pass(outs)
     ordered(ag, gb, 0)
     ordered(au, ub, 0)

time: 162 us -> 162 us (level)
  no operation moved by 1% of the time
where the time goes in v6:
time: 162 us; the launch traced here: 160 us
  Pallas kernels  159 us (98%)
    pallas_call x1, Pallas kernels, per_device(): pl.pallas_call(moe_kernel, out_shape=[pltpu.VMEM(w.shape, BF16) for w in...  155 us
    pallas_call x1, Pallas kernels, per_device(): pl.pallas_call(last_kernel, out_shape=[shape((64, 2048), BF16), shape((64...  4.31 us

profile of v6, /device:TPU:7, one launch (start us, length us, event | category | flops | bytes accessed | tf_op | source)
XLA Modules:
  0.0 160.0 jit_solution(3543307450250819029)
XLA Ops:
  0.6 154.9 %shard_map.118 = (bf16[2048,768]{1,0:T(8,128)(2,1)S(1)}, bf16[2048,768]{1,0:T(8,128)(2,1)S(1)}, bf16[768,2048]{1,0:T(8,128)(2,1)S(1)}, bf16[6,128,768]{2,1,0:T(8...) custom-call(bf16[64,2048]{1,0:T(8,128)(2,1)} %tok.1, ...), custom_call_target="tpu_custom_call" | custom-call | tf_op jit(solution)/shard_map/pallas_call | solution.py:601
  155.5 4.3 %shard_map.119 = (bf16[64,2048]{1,0:T(8,128)(2,1)}, bf16[64,2048]{1,0:T(8,128)(2,1)}, f32[8,64]{1,0:T(8,128)}, bf16[2048,768]{1,0:T(8,128)(2,1)}, bf16[2048,768]{1,0:T(8,128)(2,1)}, /*index=5*/bf16[768,2048]{1,0:T(8,128)(2,1)}) custom-call(bf16[4,64,768]{2,1,0:T(8,128)(2,1)} %get-tuple-element.22.refs_0_, bf16[4,64,640]{2,1,0:T(8,128)(2,1)} %get-tuple-element.23.refs_1_, ...), custom_call_target="tpu_custom_call" | custom-call | tf_op jit(solution)/shard_map/pallas_call | solution.py:617
